TPU v7x, 32 devices: a whole 2x2x4 slice. The times are simulated.
32 devices in a mesh: dp: 8 (over y, x, core), tensor: 4 (over z).
Axes of the slice: x: 2, y: 2, z: 4, core: 2. Of those that a mesh axis runs over, the one named last changes fastest.
Arguments:
- layer_input: bfloat16 [8, 512, 1024], P('dp', 'tensor'), may hold values from -6 to 6
- qkv_weight: bfloat16 [1024, 3072], P('dp', 'tensor'), may hold values from -0.1875 to 0.1875
- query_bias: float32 [1024], replicated, may hold values from -3 to 3
- value_bias: float32 [1024], replicated, may hold values from -3 to 3
- out_weight: bfloat16 [1024, 1024], P('tensor', 'dp'), may hold values from -1.5 to 1.5
- out_bias: float32 [1024], replicated, may hold values from -3 to 3
- attn_norm_gain: float32 [1024], replicated, may hold values from 0.5 to 1.5
- attn_norm_bias: float32 [1024], replicated, may hold values from -3 to 3
- ffn_in_weight: bfloat16 [1024, 4096], P('dp', 'tensor'), may hold values from -0.1875 to 0.1875
- ffn_in_bias: float32 [4096], replicated, may hold values from -3 to 3
- ffn_out_weight: bfloat16 [4096, 1024], P('tensor', 'dp'), may hold values from -0.09375 to 0.09375
- ffn_out_bias: float32 [1024], replicated, may hold values from -3 to 3
- ffn_norm_gain: float32 [1024], replicated, may hold values from 0.5 to 1.5
- ffn_norm_bias: float32 [1024], replicated, may hold values from -3 to 3
- grad_output: bfloat16 [8, 512, 1024], P('dp', 'tensor'), may hold values from -6 to 6
Outputs:
- layer_output: bfloat16 [8, 512, 1024], P('dp', 'tensor')
- grad_input: bfloat16 [8, 512, 1024], P('dp', 'tensor')
- grad_qkv_weight: float32 [1024, 3072], P('dp', 'tensor')
- grad_query_bias: float32 [1024], replicated
- grad_value_bias: float32 [1024], replicated
- grad_out_weight: float32 [1024, 1024], P('tensor', 'dp')
- grad_out_bias: float32 [1024], replicated
- grad_attn_norm_gain: float32 [1024], replicated
- grad_attn_norm_bias: float32 [1024], replicated
- grad_ffn_in_weight: float32 [1024, 4096], P('dp', 'tensor')
- grad_ffn_in_bias: float32 [4096], replicated
- grad_ffn_out_weight: float32 [4096, 1024], P('tensor', 'dp')
- grad_ffn_out_bias: float32 [1024], replicated
- grad_ffn_norm_gain: float32 [1024], replicated
- grad_ffn_norm_bias: float32 [1024], replicated
All inputs are finite; a program needn't handle non-finite values.
Results may differ from a plain program's by a relative error of at most 0.02.
Values may be sent and summed in bfloat16 or wider, within the bound.
A program may use at most 64 MiB of HBM per device.

v0:
```python
import jax
import jax.numpy as jnp
from jax import lax
from jax.sharding import PartitionSpec as P

HEADS = 16
HD = 64
FF = 4096


norm_eps = 1e-05
root_half = 0.7071067811865476
inv_root_tau = 0.3989422804014327


def matmul(first_op, second_op):
    return jnp.dot(first_op, second_op, preferred_element_type=jnp.float32)


def matmul_by_transpose(first_op, second_op):
    return lax.dot_general(
        first_op, second_op, (((1,), (1,)), ((), ())), preferred_element_type=jnp.float32
    )


def transpose_matmul(first_op, second_op):
    return lax.dot_general(
        first_op, second_op, (((0,), (0,)), ((), ())), preferred_element_type=jnp.float32
    )


def norm_forward(residual, norm_gain, offset):
    center = residual - jnp.mean(residual, axis=-1, keepdims=True)
    variance = jnp.mean(center * center, axis=-1, keepdims=True)
    inv_std = lax.rsqrt(variance + norm_eps)
    normed = center * inv_std
    return (normed * norm_gain + offset, normed, inv_std)


def norm_backward(upstream, normed, inv_std, norm_gain):
    scaled = upstream * norm_gain
    centered = scaled - jnp.mean(scaled, axis=-1, keepdims=True)
    return inv_std * (centered - normed * jnp.mean(scaled * normed, axis=-1, keepdims=True))


def gelu_exact(preact):
    return 0.5 * preact * (1.0 + lax.erf(preact * root_half))


def gelu_slope(preact):
    return (
        0.5 * (1.0 + lax.erf(preact * root_half))
        + preact * jnp.exp(-0.5 * preact * preact) * inv_root_tau
    )


def attend(operands):
    queries, key_rows, values = operands
    scores = jnp.einsum(
        "qhe,khe->hqk", queries, key_rows, preferred_element_type=jnp.float32
    ) * HD ** (-0.5)
    row_max = jnp.max(scores, axis=-1, keepdims=True)
    shifted = jnp.exp(scores - row_max)
    row_total = jnp.sum(shifted, axis=-1, keepdims=True)
    probs = (shifted / row_total).astype(jnp.bfloat16)
    attended = jnp.einsum("hqk,khe->qhe", probs, values, preferred_element_type=jnp.float32).astype(
        jnp.bfloat16
    )
    return (attended, row_max + jnp.log(row_total))


def attend_back(operands):
    queries, key_rows, values, log_total, grad_attended = operands
    scores = jnp.einsum(
        "qhe,khe->hqk", queries, key_rows, preferred_element_type=jnp.float32
    ) * HD ** (-0.5)
    probs = jnp.exp(scores - log_total)
    grad_probs = jnp.einsum(
        "qhe,khe->hqk", grad_attended, values, preferred_element_type=jnp.float32
    )
    grad_values = jnp.einsum(
        "hqk,qhe->khe",
        probs.astype(jnp.bfloat16),
        grad_attended,
        preferred_element_type=jnp.float32,
    ).astype(jnp.bfloat16)
    row_dot = jnp.sum(probs * grad_probs, axis=-1, keepdims=True)
    grad_scores = (probs * (grad_probs - row_dot)).astype(jnp.bfloat16)
    grad_queries = (
        jnp.einsum("hqk,khe->qhe", grad_scores, key_rows, preferred_element_type=jnp.float32)
        * HD ** (-0.5)
    ).astype(jnp.bfloat16)
    grad_keys = (
        jnp.einsum("hqk,qhe->khe", grad_scores, queries, preferred_element_type=jnp.float32)
        * HD ** (-0.5)
    ).astype(jnp.bfloat16)
    return (grad_queries, grad_keys, grad_values)


def body(
    layer_input,
    qkv_weight,
    query_bias,
    value_bias,
    out_weight,
    out_bias,
    attn_norm_gain,
    attn_norm_bias,
    ffn_in_weight,
    ffn_in_bias,
    ffn_out_weight,
    ffn_out_bias,
    ffn_norm_gain,
    ffn_norm_bias,
    grad_output,
):
    tensor_parts = lax.axis_size("tensor")
    tensor_rank = lax.axis_index("tensor")
    heads_here = HEADS // tensor_parts
    width_here = heads_here * HD
    hidden_here = FF // tensor_parts
    qkv_full, ffn_in_full, out_full, ffn_out_full = (
        lax.all_gather(qkv_weight, "dp", axis=0, tiled=True),
        lax.all_gather(ffn_in_weight, "dp", axis=0, tiled=True),
        lax.all_gather(out_weight, "dp", axis=1, tiled=True),
        lax.all_gather(ffn_out_weight, "dp", axis=1, tiled=True),
    )
    seq_count, piece_len, feature_count = layer_input.shape
    length = piece_len * tensor_parts
    row_count = seq_count * length
    input_full = lax.all_gather(layer_input, "tensor", axis=1, tiled=True)
    input_rows = input_full.reshape(row_count, feature_count)
    packed = matmul(input_rows, qkv_full).reshape(seq_count, length, heads_here, 3, HD)
    query_slice = lax.dynamic_slice_in_dim(
        query_bias.reshape(HEADS, HD), tensor_rank * heads_here, heads_here, 0
    )
    value_slice = lax.dynamic_slice_in_dim(
        value_bias.reshape(HEADS, HD), tensor_rank * heads_here, heads_here, 0
    )
    queries = (packed[:, :, :, 0] + query_slice).astype(jnp.bfloat16)
    key_rows = packed[:, :, :, 1].astype(jnp.bfloat16)
    values = (packed[:, :, :, 2] + value_slice).astype(jnp.bfloat16)
    attended, log_total = lax.map(attend, (queries, key_rows, values))
    attended_rows = attended.reshape(row_count, width_here)
    attn_part = matmul(attended_rows, out_full).reshape(seq_count, length, feature_count)
    attn_branch = (
        lax.psum_scatter(
            attn_part.astype(jnp.bfloat16), "tensor", scatter_dimension=1, tiled=True
        ).astype(jnp.float32)
        + out_bias
    )
    normed_one, unit_one, inv_std_one = norm_forward(
        layer_input.astype(jnp.float32) + attn_branch, attn_norm_gain, attn_norm_bias
    )
    normed_low = normed_one.astype(jnp.bfloat16)
    normed_full = lax.all_gather(normed_low, "tensor", axis=1, tiled=True)
    normed_rows = normed_full.reshape(row_count, feature_count)
    inner_bias = lax.dynamic_slice_in_dim(ffn_in_bias, tensor_rank * hidden_here, hidden_here, 0)
    inner_pre = matmul(normed_rows, ffn_in_full) + inner_bias
    activated = gelu_exact(inner_pre).astype(jnp.bfloat16)
    ffn_part = matmul(activated, ffn_out_full).reshape(seq_count, length, feature_count)
    ffn_branch = (
        lax.psum_scatter(
            ffn_part.astype(jnp.bfloat16), "tensor", scatter_dimension=1, tiled=True
        ).astype(jnp.float32)
        + ffn_out_bias
    )
    output_f32, unit_two, inv_std_two = norm_forward(
        normed_low.astype(jnp.float32) + ffn_branch, ffn_norm_gain, ffn_norm_bias
    )
    layer_output = output_f32.astype(jnp.bfloat16)
    grad_top = grad_output.astype(jnp.float32)
    grad_ffn_norm_gain = jnp.sum(grad_top * unit_two, axis=(0, 1))
    grad_ffn_norm_bias = jnp.sum(grad_top, axis=(0, 1))
    grad_resid_two = norm_backward(grad_top, unit_two, inv_std_two, ffn_norm_gain)
    grad_branch_two = grad_resid_two.astype(jnp.bfloat16)
    grad_ffn_out_bias = jnp.sum(grad_branch_two.astype(jnp.float32), axis=(0, 1))
    branch_two_full = lax.all_gather(grad_branch_two, "tensor", axis=1, tiled=True)
    branch_two_rows = branch_two_full.reshape(row_count, feature_count)
    grad_activated = matmul_by_transpose(branch_two_rows, ffn_out_full).astype(jnp.bfloat16)
    grad_ffn_out_local = transpose_matmul(activated, branch_two_rows)
    grad_inner = (grad_activated.astype(jnp.float32) * gelu_slope(inner_pre)).astype(jnp.bfloat16)
    inner_bias_grad = jnp.sum(grad_inner.astype(jnp.float32), axis=0)
    grad_ffn_in_local = transpose_matmul(normed_rows, grad_inner)
    normed_part = matmul_by_transpose(grad_inner, ffn_in_full).reshape(
        seq_count, length, feature_count
    )
    grad_normed = (
        lax.psum_scatter(
            normed_part.astype(jnp.bfloat16), "tensor", scatter_dimension=1, tiled=True
        ).astype(jnp.float32)
        + grad_resid_two
    )
    grad_attn_norm_gain = jnp.sum(grad_normed * unit_one, axis=(0, 1))
    grad_attn_norm_bias = jnp.sum(grad_normed, axis=(0, 1))
    grad_resid_one = norm_backward(grad_normed, unit_one, inv_std_one, attn_norm_gain)
    grad_branch_one = grad_resid_one.astype(jnp.bfloat16)
    grad_out_bias = jnp.sum(grad_branch_one.astype(jnp.float32), axis=(0, 1))
    branch_one_full = lax.all_gather(grad_branch_one, "tensor", axis=1, tiled=True)
    branch_one_rows = branch_one_full.reshape(row_count, feature_count)
    grad_attended = (
        matmul_by_transpose(branch_one_rows, out_full)
        .astype(jnp.bfloat16)
        .reshape(seq_count, length, heads_here, HD)
    )
    grad_out_local = transpose_matmul(attended_rows, branch_one_rows)
    grad_queries, grad_keys, grad_values = lax.map(
        attend_back, (queries, key_rows, values, log_total, grad_attended)
    )
    grad_packed = jnp.stack((grad_queries, grad_keys, grad_values), axis=3).reshape(
        row_count, 3 * width_here
    )
    grad_qkv_local = transpose_matmul(input_rows, grad_packed)
    input_part = matmul_by_transpose(grad_packed, qkv_full).reshape(
        seq_count, length, feature_count
    )
    grad_input = (
        lax.psum_scatter(
            input_part.astype(jnp.bfloat16), "tensor", scatter_dimension=1, tiled=True
        ).astype(jnp.float32)
        + grad_resid_one
    ).astype(jnp.bfloat16)
    grad_qkv_weight, grad_ffn_in_weight, grad_out_weight, grad_ffn_out_weight = (
        lax.psum_scatter(grad_qkv_local, "dp", scatter_dimension=0, tiled=True),
        lax.psum_scatter(grad_ffn_in_local, "dp", scatter_dimension=0, tiled=True),
        lax.psum_scatter(grad_out_local, "dp", scatter_dimension=1, tiled=True),
        lax.psum_scatter(grad_ffn_out_local, "dp", scatter_dimension=1, tiled=True),
    )
    query_grad_here = jnp.sum(grad_queries.astype(jnp.float32), axis=(0, 1)).reshape(width_here)
    value_grad_here = jnp.sum(grad_values.astype(jnp.float32), axis=(0, 1)).reshape(width_here)
    query_padded = lax.dynamic_update_slice_in_dim(
        jnp.zeros((HEADS * HD,), jnp.float32), query_grad_here, tensor_rank * width_here, 0
    )
    value_padded = lax.dynamic_update_slice_in_dim(
        jnp.zeros((HEADS * HD,), jnp.float32), value_grad_here, tensor_rank * width_here, 0
    )
    inner_padded = lax.dynamic_update_slice_in_dim(
        jnp.zeros((FF,), jnp.float32), inner_bias_grad, tensor_rank * hidden_here, 0
    )
    summed = lax.psum(
        (
            query_padded,
            value_padded,
            grad_out_bias,
            grad_attn_norm_gain,
            grad_attn_norm_bias,
            inner_padded,
            grad_ffn_out_bias,
            grad_ffn_norm_gain,
            grad_ffn_norm_bias,
        ),
        ("dp", "tensor"),
    )
    return (
        layer_output,
        grad_input,
        grad_qkv_weight,
        summed[0],
        summed[1],
        grad_out_weight,
        summed[2],
        summed[3],
        summed[4],
        grad_ffn_in_weight,
        summed[5],
        grad_ffn_out_weight,
        summed[6],
        summed[7],
        summed[8],
    )


def solution(mesh):
    placed = (
        P("dp", "tensor", None),
        P("dp", "tensor"),
        P(),
        P(),
        P("tensor", "dp"),
        P(),
        P(),
        P(),
        P("dp", "tensor"),
        P(),
        P("tensor", "dp"),
        P(),
        P(),
        P(),
        P("dp", "tensor", None),
    )
    return jax.shard_map(
        body,
        mesh=mesh,
        in_specs=placed,
        out_specs=(
            P("dp", "tensor", None),
            P("dp", "tensor", None),
            P("dp", "tensor"),
            P(),
            P(),
            P("tensor", "dp"),
            P(),
            P(),
            P(),
            P("dp", "tensor"),
            P(),
            P("tensor", "dp"),
            P(),
            P(),
            P(),
        ),
        check_vma=False,
    )
```

profile of v0, /device:TPU:0, one launch (start us, length us, event | category | flops | bytes accessed | tf_op | source)
XLA Modules:
  0.0 564.5 jit_solution(13765038207048303689)
XLA Ops:
  10.2 11.7 %all_gather.26 = bf16[256,1024]{1,0:T(8,128)(2,1)S(1)} all-gather(bf16[256,128]{1,0:T(8,128)(2,1)} %param.19), channel_id=1, replica_groups=mesh['dp'=8,'tensor'=4] {'dp'}, dimensions={1}, use_global_device_ids=true | all-gather | bytes 589824 | tf_op jit(solution)/shard_map/all_gather | solution.py:125
  22.0 16.4 %all-gather.10.cloned.1.call-done = bf16[1024,768]{1,0:T(8,128)(2,1)} async-done(((bf16[128,768]{1,0:T(8,128)(2,1)}), bf16[1024,768]{1,0:T(8,128)(2,1)}) %all-gather.10.cloned.1.call-update) | async-done | bytes 1572880 | tf_op jit(solution)/shard_map/all_gather | solution.py:123
  38.3 2.6 copy.36
  40.9 26.9 %all-gather.8.cloned.1.call-done = bf16[1,512,1024]{2,1,0:T(8,128)(2,1)} async-done(((bf16[1,128,1024]{2,1,0:T(8,128)(2,1)}), bf16[1,512,1024]{2,1,0:T(8,128)(2,1)}) %all-gather.8.cloned.1.call-update) | async-done | bytes 1048592 | tf_op jit(solution)/shard_map/all_gather | solution.py:131
  67.9 2.7 convolution_bitcast_fusion.1
  72.1 1.2 copy-done
  73.3 1.0 fusion.22
  74.4 1.5 fusion.14
  76.5 26.2 %reduce-scatter.9.cloned.1.call-done = bf16[1,128,1024]{2,1,0:T(8,128)(2,1)} async-done(((bf16[1,512,1024]{2,1,0:T(8,128)(2,1)}), bf16[1,128,1024]{2,1,0:T(8,128)(2,1)}) %reduce-scatter.9.cloned.1.call-update) | async-done | bytes 262160 | tf_op jit(solution)/shard_map/reduce_scatter | solution.py:147
  102.7 1.1 fusion.47
  103.8 1.2 multiply_reduce_fusion.5
  105.0 1.8 add_convert_fusion.2
  108.1 23.0 %all-gather.14.cloned.1.call-done = bf16[1024,1024]{1,0:T(8,128)(2,1)} async-done(((bf16[128,1024]{1,0:T(8,128)(2,1)}), bf16[1024,1024]{1,0:T(8,128)(2,1)}) %all-gather.14.cloned.1.call-update) | async-done | bytes 2097168 | tf_op jit(solution)/shard_map/all_gather | solution.py:124
  131.1 30.0 %all-gather.12.cloned.1.call-done = bf16[1,512,1024]{2,1,0:T(8,128)(2,1)} async-done(((bf16[1,128,1024]{2,1,0:T(8,128)(2,1)}), bf16[1,512,1024]{2,1,0:T(8,128)(2,1)}) %all-gather.12.cloned.1.call-update) | async-done | bytes 1048592 | tf_op jit(solution)/shard_map/all_gather | solution.py:156
  161.2 5.0 multiply_convert_fusion.1
  166.1 24.6 %all-gather.16.cloned.1.call-done = bf16[1024,1024]{1,0:T(8,128)(2,1)} async-done(((bf16[1024,128]{1,0:T(8,128)(2,1)}), bf16[1024,1024]{1,0:T(8,128)(2,1)}) %all-gather.16.cloned.1.call-update) | async-done | bytes 2097168 | tf_op jit(solution)/shard_map/all_gather | solution.py:126
  190.8 4.2 fusion.15
  195.1 27.2 %reduce-scatter.11.cloned.1.call-done = bf16[1,128,1024]{2,1,0:T(8,128)(2,1)} async-done(((bf16[1,512,1024]{2,1,0:T(8,128)(2,1)}), bf16[1,128,1024]{2,1,0:T(8,128)(2,1)}) %reduce-scatter.11.cloned.1.call-update) | async-done | bytes 262160 | tf_op jit(solution)/shard_map/reduce_scatter | solution.py:163
  222.3 1.1 fusion.48
  223.5 1.2 multiply_reduce_fusion.4
  224.6 1.3 fusion.42
  226.0 2.1 convert_reduce_fusion.2
  228.2 26.7 %all-gather.18.cloned.1.call-done = bf16[1,512,1024]{2,1,0:T(8,128)(2,1)} async-done(((bf16[1,128,1024]{2,1,0:T(8,128)(2,1)}), bf16[1,512,1024]{2,1,0:T(8,128)(2,1)}) %all-gather.18.cloned.1.call-update) | async-done | bytes 1048592 | tf_op jit(solution)/shard_map/all_gather | solution.py:178
  254.9 4.6 convert_reduce_fusion
  260.5 2.3 fusion.16
  263.0 26.6 %reduce-scatter.13.cloned.1.call-done = bf16[1,128,1024]{2,1,0:T(8,128)(2,1)} async-done(((bf16[1,512,1024]{2,1,0:T(8,128)(2,1)}), bf16[1,128,1024]{2,1,0:T(8,128)(2,1)}) %reduce-scatter.13.cloned.1.call-update) | async-done | bytes 262160 | tf_op jit(solution)/shard_map/reduce_scatter | solution.py:189
  289.6 1.3 multiply_reduce_fusion.2
  290.9 2.1 convert_reduce_fusion.3
  293.1 26.7 %all-gather.20.cloned.1.call-done = bf16[1,512,1024]{2,1,0:T(8,128)(2,1)} async-done(((bf16[1,128,1024]{2,1,0:T(8,128)(2,1)}), bf16[1,512,1024]{2,1,0:T(8,128)(2,1)}) %all-gather.20.cloned.1.call-update) | async-done | bytes 1048592 | tf_op jit(solution)/shard_map/all_gather | solution.py:199
  319.7 1.7 convolution_convert_fusion.5
  321.5 3.3 convert_reduce_fusion.4
  324.9 1.2 multiply_reduce_fusion
  326.1 1.2 multiply_convert_fusion
  328.8 1.2 copy-done.8
  330.0 2.0 fusion.13
  332.1 2.7 convolution_bitcast_fusion
  335.0 1.1 copy-done.9
  336.1 1.4 fusion.25
  337.6 3.2 fusion.28
  340.9 1.1 copy-done.6
  342.4 3.3 fusion.31
  346.5 41.5 %all-reduce = (f32[1024]{0:T(1024)}, f32[1024]{0:T(1024)}, f32[1024]{0:T(1024)}, f32[1024]{0:T(1024)}, f32[1024]{0:T(1024)}, /*index=5*/f32[4096]{0:T(1024)}, f32[1024]{0:T(1024)}, f32[1024]{0:T(1024)}, f32[1024]{0:T(1024)}) all-reduce(f32[1024]{0:T(1024)S(1)} %dynamic_update_slice.21, ...), channel_id=1, replica_groups=mesh['dp'=8,'tensor'=4] {'dp','tensor'}, use_global_device_ids=true, to_apply=%region_17.18 | all-reduce | flops 12288 | bytes 98304 | tf_op jit(solution)/shard_map/psum | solution.py:240
  388.0 1.7 add_convert_fusion
  389.7 17.5 %reduce-scatter.17.cloned.1.call-done = f32[128,768]{0,1:T(8,128)} async-done(((f32[1024,768]{0,1:T(8,128)}), f32[128,768]{0,1:T(8,128)}) %reduce-scatter.17.cloned.1.call-update) | async-done | bytes 393232 | tf_op jit(solution)/shard_map/reduce_scatter | solution.py:224
  407.2 1.9 copy.42
  409.1 38.2 %reduce-scatter.19.cloned.1.call-done = f32[256,128]{1,0:T(8,128)} async-done(((f32[256,1024]{1,0:T(8,128)}), f32[256,128]{1,0:T(8,128)}) %reduce-scatter.19.cloned.1.call-update) | async-done | bytes 131088 | tf_op jit(solution)/shard_map/reduce_scatter | solution.py:226
  447.4 55.5 %reduce-scatter.23.cloned.1.call-done = f32[1024,128]{1,0:T(8,128)} async-done(((f32[1024,1024]{1,0:T(8,128)}), f32[1024,128]{1,0:T(8,128)}) %reduce-scatter.23.cloned.1.call-update) | async-done | bytes 524304 | tf_op jit(solution)/shard_map/reduce_scatter | solution.py:227
  502.9 55.1 %reduce-scatter.21.cloned.1.call-done = f32[128,1024]{1,0:T(8,128)} async-done(((f32[1024,1024]{1,0:T(8,128)}), f32[128,1024]{1,0:T(8,128)}) %reduce-scatter.21.cloned.1.call-update) | async-done | bytes 524304 | tf_op jit(solution)/shard_map/reduce_scatter | solution.py:225
  (98 shorter events, 11.1 us)
Async XLA Ops:
  7.2 31.1 %all-gather.10.cloned.1.call-start = ((), (), s32[]{:S(2)}) async-start(), calls=%async_computation.9 | async-start | bytes 1769472 | tf_op jit(solution)/shard_map/all_gather | solution.py:123
  7.9 59.9 %all-gather.8.cloned.1.call-start = ((), (), s32[]{:S(2)}) async-start(), calls=%async_computation.8 | async-start | bytes 1310720 | tf_op jit(solution)/shard_map/all_gather | solution.py:131
  8.7 94.0 %reduce-scatter.9.cloned.1.call-start = ((), (), s32[]{:S(2)}) async-start(), calls=%async_computation.10 | async-start | bytes 1310720 | tf_op jit(solution)/shard_map/reduce_scatter | solution.py:147
  71.4 1.9 copy-start
  74.3 28.3 %copy-start.2 = (bf16[1,128,1024]{2,1,0:T(8,128)(2,1)S(1)}, bf16[1,128,1024]{2,1,0:T(8,128)(2,1)}, u32[]{:S(2)}) copy-start(bf16[1,128,1024]{2,1,0:T(8,128)(2,1)} %param.15) | copy-start | bytes 786436
  74.3 28.3 %copy-start.15 = (f32[1024]{0:T(1024)S(1)}, f32[1024]{0:T(1024)}, u32[]{:S(2)}) copy-start(f32[1024]{0:T(1024)} %param.20) | copy-start | bytes 12292
  74.3 30.6 %copy-start.17 = (f32[1024]{0:T(1024)S(1)}, f32[1024]{0:T(1024)}, u32[]{:S(2)}) copy-start(f32[1024]{0:T(1024)} %param.21) | copy-start | bytes 12292
  74.4 30.6 %copy-start.19 = (f32[1024]{0:T(1024)S(1)}, f32[1024]{0:T(1024)}, u32[]{:S(2)}) copy-start(f32[1024]{0:T(1024)} %param.22) | copy-start | bytes 12292
  75.9 55.3 %all-gather.14.cloned.1.call-start = ((), (), s32[]{:S(2)}) async-start(), calls=%async_computation.12 | async-start | bytes 2359296 | tf_op jit(solution)/shard_map/all_gather | solution.py:124
  76.4 84.7 %all-gather.12.cloned.1.call-start = ((), (), s32[]{:S(2)}) async-start(), calls=%async_computation.11 | async-start | bytes 1310720 | tf_op jit(solution)/shard_map/all_gather | solution.py:156
  106.8 84.0 %all-gather.16.cloned.1.call-start = ((), (), s32[]{:S(2)}) async-start(), calls=%async_computation.13 | async-start | bytes 2359296 | tf_op jit(solution)/shard_map/all_gather | solution.py:126
  107.4 114.9 %reduce-scatter.11.cloned.1.call-start = ((), (), s32[]{:S(2)}) async-start(), calls=%async_computation.14 | async-start | bytes 1310720 | tf_op jit(solution)/shard_map/reduce_scatter | solution.py:163
  190.8 31.5 %copy-start.3 = (bf16[1,128,1024]{2,1,0:T(8,128)(2,1)S(1)}, bf16[1,128,1024]{2,1,0:T(8,128)(2,1)}, u32[]{:S(2)}) copy-start(bf16[1,128,1024]{2,1,0:T(8,128)(2,1)} %add_convert_fusion.2) | copy-start | bytes 786436
  190.8 31.5 %copy-start.16 = (f32[1024]{0:T(1024)S(1)}, f32[1024]{0:T(1024)}, u32[]{:S(2)}) copy-start(f32[1024]{0:T(1024)} %param.26) | copy-start | bytes 12292
  195.0 29.6 %copy-start.10 = (bf16[1,128,1024]{2,1,0:T(8,128)(2,1)S(1)}, bf16[1,128,1024]{2,1,0:T(8,128)(2,1)}, u32[]{:S(2)}) copy-start(bf16[1,128,1024]{2,1,0:T(8,128)(2,1)} %param.29) | copy-start | bytes 786436
  195.0 29.6 %copy-start.18 = (f32[1024]{0:T(1024)S(1)}, f32[1024]{0:T(1024)}, u32[]{:S(2)}) copy-start(f32[1024]{0:T(1024)} %param.27) | copy-start | bytes 12292
  195.0 30.9 %copy-start.20 = (f32[1024]{0:T(1024)S(1)}, f32[1024]{0:T(1024)}, u32[]{:S(2)}) copy-start(f32[1024]{0:T(1024)} %param.28) | copy-start | bytes 12292
  195.0 59.8 %all-gather.18.cloned.1.call-start = ((), (), s32[]{:S(2)}) async-start(), calls=%async_computation.15 | async-start | bytes 1310720 | tf_op jit(solution)/shard_map/all_gather | solution.py:178
  228.1 61.4 %reduce-scatter.13.cloned.1.call-start = ((), (), s32[]{:S(2)}) async-start(), calls=%async_computation.16 | async-start | bytes 1310720 | tf_op jit(solution)/shard_map/reduce_scatter | solution.py:189
  254.9 5.6 copy-start.21
  259.4 1.0 copy-start.12
  260.5 29.1 %copy-start.4 = (bf16[1,128,1024]{2,1,0:T(8,128)(2,1)S(1)}, bf16[1,128,1024]{2,1,0:T(8,128)(2,1)}, u32[]{:S(2)}) copy-start(bf16[1,128,1024]{2,1,0:T(8,128)(2,1)} %reduce-scatter.9.cloned.1.call-done) | copy-start | bytes 786436
  262.8 57.0 %all-gather.20.cloned.1.call-start = ((), (), s32[]{:S(2)}) async-start(), calls=%async_computation.17 | async-start | bytes 1310720 | tf_op jit(solution)/shard_map/all_gather | solution.py:199
  293.0 95.0 %reduce-scatter.15.cloned.1.call-start = ((), (), s32[]{:S(2)}) async-start(), calls=%async_computation.18 | async-start | bytes 1310720 | tf_op jit(solution)/shard_map/reduce_scatter | solution.py:218
  321.4 3.5 copy-start.1
  328.6 1.4 copy-start.8
  330.0 2.1 copy-start.11
  332.1 75.1 %reduce-scatter.17.cloned.1.call-start = ((), (), s32[]{:S(2)}) async-start(), calls=%async_computation.19 | async-start | bytes 3538944 | tf_op jit(solution)/shard_map/reduce_scatter | solution.py:224
  334.9 1.2 copy-start.9
  334.9 2.7 copy-start.7
  334.9 2.7 copy-start.14
  334.9 112.4 %reduce-scatter.19.cloned.1.call-start = ((), (), s32[]{:S(2)}) async-start(), calls=%async_computation.20 | async-start | bytes 1179648 | tf_op jit(solution)/shard_map/reduce_scatter | solution.py:226
  337.5 165.3 %reduce-scatter.23.cloned.1.call-start = ((), (), s32[]{:S(2)}) async-start(), calls=%async_computation.22 | async-start | bytes 4718592 | tf_op jit(solution)/shard_map/reduce_scatter | solution.py:227
  340.8 1.2 copy-start.6
  340.8 1.5 copy-start.13
  340.9 217.1 %reduce-scatter.21.cloned.1.call-start = ((), (), s32[]{:S(2)}) async-start(), calls=%async_computation.21 | async-start | bytes 4718592 | tf_op jit(solution)/shard_map/reduce_scatter | solution.py:225
  345.6 42.4 %copy-start.5 = (f32[1,128,1024]{2,1,0:T(8,128)S(1)}, f32[1,128,1024]{2,1,0:T(8,128)}, u32[]{:S(2)}) copy-start(f32[1,128,1024]{2,1,0:T(8,128)} %get-tuple-element.112) | copy-start | bytes 1572868
Sparse Core Ops, SparseCore 0:
  9.9 28.3 all-gather.9
  39.9 27.9 all-gather.7
  76.0 26.6 reduce-scatter.8
  104.6 26.5 all-gather.13
  133.2 27.9 all-gather.11
  163.1 27.6 all-gather.15
  195.2 27.1 reduce-scatter.10
  228.2 26.5 all-gather.17
  262.9 26.6 reduce-scatter.12
  293.1 26.5 all-gather.19
  332.2 26.6 reduce-scatter.14
  362.1 45.0 reduce-scatter.16
  411.3 36.0 reduce-scatter.18
  451.5 51.2 reduce-scatter.22
  506.6 51.3 reduce-scatter.20
where the time goes:
time: 565 us
  waiting for transfers between devices  423 us (75%)
  blocking collectives  53.2 us (9%)
  matrix products  42.2 us (7%)
  other arithmetic  17 us (3%)
  between operations  14.2 us (3%)
  local copies, waits for them, and re-layouts  13.9 us (2%)
    reduce_scatter x1, waiting for transfers between devices, body(): lax.psum_scatter(grad_ffn_out_local, 'dp', scatter_dimension=1, tiled=True)  55.5 us
    reduce_scatter x1, waiting for transfers between devices, body(): lax.psum_scatter(grad_ffn_in_local, 'dp', scatter_dimension=0, tiled=True)  55.1 us
    psum x1, blocking collectives, body(): lax.psum((query_padded, value_padded, grad_out_bias, grad_attn_norm_gain,...  41.5 us
    reduce_scatter x1, waiting for transfers between devices, body(): lax.psum_scatter(grad_out_local, 'dp', scatter_dimension=1, tiled=True)  38.2 us
    all_gather x1, waiting for transfers between devices, body(): normed_full = lax.all_gather(normed_low, 'tensor', axis=1, tiled=True)  30 us
    reduce_scatter x1, waiting for transfers between devices, body(): lax.psum_scatter(ffn_part.astype(jnp.bfloat16), 'tensor', scatter_dimensi...  27.2 us
    all_gather x1, waiting for transfers between devices, body(): input_full = lax.all_gather(layer_input, 'tensor', axis=1, tiled=True)  26.9 us
    all_gather x1, waiting for transfers between devices, body(): lax.all_gather(grad_branch_two, 'tensor', axis=1, tiled=True)  26.7 us
  transfers between devices with their start and end apart: 15, of which 14 were waited for; matrix products, arithmetic and copies ran while one was open for 5% of the time, Pallas kernels for 0%

commit v1 on v0

--- a/solution.py
+++ b/solution.py
@@ -178,7 +178,7 @@
     branch_two_full = lax.all_gather(grad_branch_two, "tensor", axis=1, tiled=True)
     branch_two_rows = branch_two_full.reshape(row_count, feature_count)
     grad_activated = matmul_by_transpose(branch_two_rows, ffn_out_full).astype(jnp.bfloat16)
-    grad_ffn_out_local = transpose_matmul(activated, branch_two_rows)
+    grad_ffn_out_local = transpose_matmul(branch_two_rows, activated)
     grad_inner = (grad_activated.astype(jnp.float32) * gelu_slope(inner_pre)).astype(jnp.bfloat16)
     inner_bias_grad = jnp.sum(grad_inner.astype(jnp.float32), axis=0)
     grad_ffn_in_local = transpose_matmul(normed_rows, grad_inner)
@@ -203,7 +203,7 @@
         .astype(jnp.bfloat16)
         .reshape(seq_count, length, heads_here, HD)
     )
-    grad_out_local = transpose_matmul(attended_rows, branch_one_rows)
+    grad_out_local = transpose_matmul(branch_one_rows, attended_rows)
     grad_queries, grad_keys, grad_values = lax.map(
         attend_back, (queries, key_rows, values, log_total, grad_attended)
     )
@@ -220,12 +220,23 @@
         ).astype(jnp.float32)
         + grad_resid_one
     ).astype(jnp.bfloat16)
-    grad_qkv_weight, grad_ffn_in_weight, grad_out_weight, grad_ffn_out_weight = (
-        lax.psum_scatter(grad_qkv_local, "dp", scatter_dimension=0, tiled=True),
-        lax.psum_scatter(grad_ffn_in_local, "dp", scatter_dimension=0, tiled=True),
-        lax.psum_scatter(grad_out_local, "dp", scatter_dimension=1, tiled=True),
-        lax.psum_scatter(grad_ffn_out_local, "dp", scatter_dimension=1, tiled=True),
-    )
+    low_kind = jnp.bfloat16
+    ffn_grads = lax.psum_scatter(
+        jnp.concatenate((grad_ffn_in_local.astype(low_kind), grad_ffn_out_local.astype(low_kind)), axis=1),
+        "dp",
+        scatter_dimension=0,
+        tiled=True,
+    ).astype(jnp.float32)
+    attn_grads = lax.psum_scatter(
+        jnp.concatenate((grad_qkv_local.astype(low_kind), grad_out_local.astype(low_kind)), axis=1),
+        "dp",
+        scatter_dimension=0,
+        tiled=True,
+    ).astype(jnp.float32)
+    grad_ffn_in_weight = ffn_grads[:, :hidden_here]
+    grad_ffn_out_weight = ffn_grads[:, hidden_here:].T
+    grad_qkv_weight = attn_grads[:, : 3 * width_here]
+    grad_out_weight = attn_grads[:, 3 * width_here :].T
     query_grad_here = jnp.sum(grad_queries.astype(jnp.float32), axis=(0, 1)).reshape(width_here)
     value_grad_here = jnp.sum(grad_values.astype(jnp.float32), axis=(0, 1)).reshape(width_here)
     query_padded = lax.dynamic_update_slice_in_dim(
@@ -237,20 +248,22 @@
     inner_padded = lax.dynamic_update_slice_in_dim(
         jnp.zeros((FF,), jnp.float32), inner_bias_grad, tensor_rank * hidden_here, 0
     )
-    summed = lax.psum(
-        (
-            query_padded,
-            value_padded,
-            grad_out_bias,
-            grad_attn_norm_gain,
-            grad_attn_norm_bias,
-            inner_padded,
-            grad_ffn_out_bias,
-            grad_ffn_norm_gain,
-            grad_ffn_norm_bias,
-        ),
-        ("dp", "tensor"),
-    )
+    small = (
+        query_padded,
+        value_padded,
+        grad_out_bias,
+        grad_attn_norm_gain,
+        grad_attn_norm_bias,
+        inner_padded,
+        grad_ffn_out_bias,
+        grad_ffn_norm_gain,
+        grad_ffn_norm_bias,
+    )
+    flat = lax.psum(jnp.concatenate(small).reshape(-1, 128), ("dp", "tensor")).reshape(-1)
+    summed, at = [], 0
+    for member in small:
+        summed.append(flat[at : at + member.shape[0]])
+        at += member.shape[0]
     return (
         layer_output,
         grad_input,

time: 565 us -> 468 us (0.83)
  waiting for transfers between devices: 423 us -> 316 us
  local copies, waits for them, and re-layouts: 13.9 us -> 26.6 us
    reduce_scatter x4 -> x0, waiting for transfers between devices: 166 us -> none  [the longest x1 55.5 us: body(): lax.psum_scatter(grad_ffn_out_local, 'dp', scatter_dimension=1, tiled=True)]
    unnamed x15, waiting for transfers between devices: 2.6 us -> 61.9 us
    unnamed x45 -> x56, local copies, waits for them, and re-layouts: 8.17 us -> 18 us
  transfers between devices with their start and end apart: 15 -> 13, of which waited for: 14 -> 12; matrix products, arithmetic and copies ran while one was open for 5% -> 8% of each run, Pallas kernels for 0% -> 0%
where the time goes in v1:
time: 468 us; the launch traced here: 467 us
  waiting for transfers between devices  316 us (68%)
  blocking collectives  52.3 us (11%)
  matrix products  37 us (8%)
  local copies, waits for them, and re-layouts  26.6 us (6%)
  other arithmetic  19.6 us (4%)
  between operations  14.3 us (3%)
    unnamed x15, waiting for transfers between devices  61.9 us
    psum x1, blocking collectives, body(): lax.psum(jnp.concatenate(small).reshape(-1, 128), ('dp', 'tensor'))  40.6 us
    all_gather x1, waiting for transfers between devices, body(): normed_full = lax.all_gather(normed_low, 'tensor', axis=1, tiled=True)  30 us
    reduce_scatter x1, waiting for transfers between devices, body(): lax.psum_scatter(ffn_part.astype(jnp.bfloat16), 'tensor', scatter_dimensi...  27.2 us
    all_gather x1, waiting for transfers between devices, body(): input_full = lax.all_gather(layer_input, 'tensor', axis=1, tiled=True)  26.9 us
    all_gather x1, waiting for transfers between devices, body(): lax.all_gather(grad_branch_two, 'tensor', axis=1, tiled=True)  26.7 us
    all_gather x1, waiting for transfers between devices, body(): lax.all_gather(grad_branch_one, 'tensor', axis=1, tiled=True)  26.7 us
    reduce_scatter x1, waiting for transfers between devices, body(): lax.psum_scatter(normed_part.astype(jnp.bfloat16), 'tensor', scatter_dime...  26.6 us
  transfers between devices with their start and end apart: 13, of which 12 were waited for; matrix products, arithmetic and copies ran while one was open for 8% of the time, Pallas kernels for 0%

profile of v1, /device:TPU:0, one launch (start us, length us, event | category | flops | bytes accessed | tf_op | source)
XLA Modules:
  0.0 467.0 jit_solution(17808091274079286854)
XLA Ops:
  10.2 11.7 %all_gather.26 = bf16[256,1024]{1,0:T(8,128)(2,1)S(1)} all-gather(bf16[256,128]{1,0:T(8,128)(2,1)} %param.19), channel_id=1, replica_groups=mesh['dp'=8,'tensor'=4] {'dp'}, dimensions={1}, use_global_device_ids=true | all-gather | bytes 589824 | tf_op jit(solution)/shard_map/all_gather | solution.py:125
  22.0 16.4 %all-gather.10.cloned.1.call-done = bf16[1024,768]{1,0:T(8,128)(2,1)} async-done(((bf16[128,768]{1,0:T(8,128)(2,1)}), bf16[1024,768]{1,0:T(8,128)(2,1)}) %all-gather.10.cloned.1.call-update) | async-done | bytes 1572880 | tf_op jit(solution)/shard_map/all_gather | solution.py:123
  38.3 2.6 copy.45
  40.9 26.9 %all-gather.8.cloned.1.call-done = bf16[1,512,1024]{2,1,0:T(8,128)(2,1)} async-done(((bf16[1,128,1024]{2,1,0:T(8,128)(2,1)}), bf16[1,512,1024]{2,1,0:T(8,128)(2,1)}) %all-gather.8.cloned.1.call-update) | async-done | bytes 1048592 | tf_op jit(solution)/shard_map/all_gather | solution.py:131
  67.9 2.7 convolution_bitcast_fusion
  72.1 1.2 copy-done
  73.3 1.0 fusion.23
  74.4 1.5 fusion.15
  76.5 26.2 %reduce-scatter.11.cloned.1.call-done = bf16[1,128,1024]{2,1,0:T(8,128)(2,1)} async-done(((bf16[1,512,1024]{2,1,0:T(8,128)(2,1)}), bf16[1,128,1024]{2,1,0:T(8,128)(2,1)}) %reduce-scatter.11.cloned.1.call-update) | async-done | bytes 262160 | tf_op jit(solution)/shard_map/reduce_scatter | solution.py:147
  102.7 1.1 fusion.45
  103.8 1.2 multiply_reduce_fusion.5
  105.0 1.8 add_convert_fusion.2
  108.1 23.0 %all-gather.14.cloned.1.call-done = bf16[1024,1024]{1,0:T(8,128)(2,1)} async-done(((bf16[128,1024]{1,0:T(8,128)(2,1)}), bf16[1024,1024]{1,0:T(8,128)(2,1)}) %all-gather.14.cloned.1.call-update) | async-done | bytes 2097168 | tf_op jit(solution)/shard_map/all_gather | solution.py:124
  131.1 30.0 %all-gather.12.cloned.1.call-done = bf16[1,512,1024]{2,1,0:T(8,128)(2,1)} async-done(((bf16[1,128,1024]{2,1,0:T(8,128)(2,1)}), bf16[1,512,1024]{2,1,0:T(8,128)(2,1)}) %all-gather.12.cloned.1.call-update) | async-done | bytes 1048592 | tf_op jit(solution)/shard_map/all_gather | solution.py:156
  161.2 5.0 %multiply_convert_fusion.1 = (bf16[512,1024]{1,0:T(8,128)(2,1)}, f32[512,1024]{1,0:T(8,128)}) fusion(f32[1024]{0:T(1024)S(1)} %dynamic_slice.29, bf16[1024,1024]{1,0:T(8,128)(2,1)} %all-gather.14.cloned.1.call-done, bf16[1,512,1024]{2,1,0:T(8,128)(2,1)} %all-gather.12.cloned.1.call-done), kind=kOutput, calls=%fused_computation.20 | convolution fusion | flops 1076887552 | bytes 6295552 | tf_op jit(solution)/shard_map/dot_general | solution.py:17
  166.1 24.6 %all-gather.16.cloned.1.call-done = bf16[1024,1024]{1,0:T(8,128)(2,1)} async-done(((bf16[1024,128]{1,0:T(8,128)(2,1)}), bf16[1024,1024]{1,0:T(8,128)(2,1)}) %all-gather.16.cloned.1.call-update) | async-done | bytes 2097168 | tf_op jit(solution)/shard_map/all_gather | solution.py:126
  190.8 4.2 fusion.16
  195.1 27.2 %reduce-scatter.13.cloned.1.call-done = bf16[1,128,1024]{2,1,0:T(8,128)(2,1)} async-done(((bf16[1,512,1024]{2,1,0:T(8,128)(2,1)}), bf16[1,128,1024]{2,1,0:T(8,128)(2,1)}) %reduce-scatter.13.cloned.1.call-update) | async-done | bytes 262160 | tf_op jit(solution)/shard_map/reduce_scatter | solution.py:163
  222.3 1.1 fusion.46
  223.5 1.2 multiply_reduce_fusion.4
  224.6 1.3 fusion.40
  226.0 2.1 convert_reduce_fusion.2
  228.2 26.7 %all-gather.18.cloned.1.call-done = bf16[1,512,1024]{2,1,0:T(8,128)(2,1)} async-done(((bf16[1,128,1024]{2,1,0:T(8,128)(2,1)}), bf16[1,512,1024]{2,1,0:T(8,128)(2,1)}) %all-gather.18.cloned.1.call-update) | async-done | bytes 1048592 | tf_op jit(solution)/shard_map/all_gather | solution.py:178
  254.9 4.6 convert_reduce_fusion
  259.5 1.0 copy-done.19
  260.5 2.3 fusion.17
  263.0 26.6 %reduce-scatter.15.cloned.1.call-done = bf16[1,128,1024]{2,1,0:T(8,128)(2,1)} async-done(((bf16[1,512,1024]{2,1,0:T(8,128)(2,1)}), bf16[1,128,1024]{2,1,0:T(8,128)(2,1)}) %reduce-scatter.15.cloned.1.call-update) | async-done | bytes 262160 | tf_op jit(solution)/shard_map/reduce_scatter | solution.py:189
  289.6 1.3 multiply_reduce_fusion.2
  290.9 2.1 convert_reduce_fusion.3
  293.1 26.7 %all-gather.20.cloned.1.call-done = bf16[1,512,1024]{2,1,0:T(8,128)(2,1)} async-done(((bf16[1,128,1024]{2,1,0:T(8,128)(2,1)}), bf16[1,512,1024]{2,1,0:T(8,128)(2,1)}) %all-gather.20.cloned.1.call-update) | async-done | bytes 1048592 | tf_op jit(solution)/shard_map/all_gather | solution.py:199
  319.7 1.7 convolution_convert_fusion.9
  321.5 3.3 convert_reduce_fusion.4
  324.9 1.2 multiply_reduce_fusion
  326.1 1.2 multiply_convert_fusion
  328.8 1.2 copy-done.6
  330.0 2.1 fusion.14
  332.2 2.7 convolution_convert_fusion
  334.9 1.3 convolution_convert_fusion.1
  336.2 2.4 pad_maximum_fusion
  338.6 6.5 %copy.60 = bf16[1024,2048]{1,0:T(8,128)(2,1)} copy(bf16[1024,2048]{0,1:T(8,128)(2,1)} %pad_maximum_fusion) | data formatting | bytes 8388608
  348.0 2.6 copy.58
  351.5 40.6 %psum.7 = f32[96,128]{1,0:T(8,128)S(1)} all-reduce(f32[96,128]{1,0:T(8,128)S(1)} %bitcast.142), channel_id=1, replica_groups=mesh['dp'=8,'tensor'=4] {'dp','tensor'}, use_global_device_ids=true, to_apply=%region_25.26 | all-reduce | flops 12288 | bytes 98304 | tf_op jit(solution)/shard_map/psum | solution.py:262
  393.4 1.7 add_convert_fusion
  395.1 17.7 %reduce-scatter.21.cloned.1.call-done = bf16[128,2048]{1,0:T(8,128)(2,1)} async-done(((bf16[1024,2048]{1,0:T(8,128)(2,1)}), bf16[128,2048]{1,0:T(8,128)(2,1)}) %reduce-scatter.21.cloned.1.call-update) | async-done | bytes 524304
  412.8 1.3 copy.61
  414.2 1.0 copy.52
  416.0 41.6 %reduce-scatter.19.cloned.1.call-done = bf16[128,1024]{1,0:T(8,128)(2,1)} async-done(((bf16[1024,1024]{1,0:T(8,128)(2,1)}), bf16[128,1024]{1,0:T(8,128)(2,1)}) %reduce-scatter.19.cloned.1.call-update) | async-done | bytes 262160
  457.7 1.1 copy.59
  (114 shorter events, 16.2 us)
Async XLA Ops:
  7.2 31.1 %all-gather.10.cloned.1.call-start = ((), (), s32[]{:S(2)}) async-start(), calls=%async_computation.7 | async-start | bytes 1769472 | tf_op jit(solution)/shard_map/all_gather | solution.py:123
  7.9 59.9 %all-gather.8.cloned.1.call-start = ((), (), s32[]{:S(2)}) async-start(), calls=%async_computation.6 | async-start | bytes 1310720 | tf_op jit(solution)/shard_map/all_gather | solution.py:131
  8.7 94.0 %reduce-scatter.11.cloned.1.call-start = ((), (), s32[]{:S(2)}) async-start(), calls=%async_computation.8 | async-start | bytes 1310720 | tf_op jit(solution)/shard_map/reduce_scatter | solution.py:147
  71.4 1.9 copy-start
  74.3 28.3 %copy-start.2 = (bf16[1,128,1024]{2,1,0:T(8,128)(2,1)S(1)}, bf16[1,128,1024]{2,1,0:T(8,128)(2,1)}, u32[]{:S(2)}) copy-start(bf16[1,128,1024]{2,1,0:T(8,128)(2,1)} %param.15) | copy-start | bytes 786436
  74.3 28.3 %copy-start.9 = (f32[1024]{0:T(1024)S(1)}, f32[1024]{0:T(1024)}, u32[]{:S(2)}) copy-start(f32[1024]{0:T(1024)} %param.20) | copy-start | bytes 12292
  74.4 30.6 %copy-start.11 = (f32[1024]{0:T(1024)S(1)}, f32[1024]{0:T(1024)}, u32[]{:S(2)}) copy-start(f32[1024]{0:T(1024)} %param.21) | copy-start | bytes 12292
  74.4 30.6 %copy-start.13 = (f32[1024]{0:T(1024)S(1)}, f32[1024]{0:T(1024)}, u32[]{:S(2)}) copy-start(f32[1024]{0:T(1024)} %param.22) | copy-start | bytes 12292
  75.9 55.3 %all-gather.14.cloned.1.call-start = ((), (), s32[]{:S(2)}) async-start(), calls=%async_computation.10 | async-start | bytes 2359296 | tf_op jit(solution)/shard_map/all_gather | solution.py:124
  76.5 84.7 %all-gather.12.cloned.1.call-start = ((), (), s32[]{:S(2)}) async-start(), calls=%async_computation.9 | async-start | bytes 1310720 | tf_op jit(solution)/shard_map/all_gather | solution.py:156
  106.8 84.0 %all-gather.16.cloned.1.call-start = ((), (), s32[]{:S(2)}) async-start(), calls=%async_computation.11 | async-start | bytes 2359296 | tf_op jit(solution)/shard_map/all_gather | solution.py:126
  107.4 114.9 %reduce-scatter.13.cloned.1.call-start = ((), (), s32[]{:S(2)}) async-start(), calls=%async_computation.12 | async-start | bytes 1310720 | tf_op jit(solution)/shard_map/reduce_scatter | solution.py:163
  190.8 31.5 %copy-start.3 = (bf16[1,128,1024]{2,1,0:T(8,128)(2,1)S(1)}, bf16[1,128,1024]{2,1,0:T(8,128)(2,1)}, u32[]{:S(2)}) copy-start(bf16[1,128,1024]{2,1,0:T(8,128)(2,1)} %add_convert_fusion.2) | copy-start | bytes 786436
  190.8 31.5 %copy-start.10 = (f32[1024]{0:T(1024)S(1)}, f32[1024]{0:T(1024)}, u32[]{:S(2)}) copy-start(f32[1024]{0:T(1024)} %param.26) | copy-start | bytes 12292
  195.0 29.6 %copy-start.8 = (bf16[1,128,1024]{2,1,0:T(8,128)(2,1)S(1)}, bf16[1,128,1024]{2,1,0:T(8,128)(2,1)}, u32[]{:S(2)}) copy-start(bf16[1,128,1024]{2,1,0:T(8,128)(2,1)} %param.29) | copy-start | bytes 786436
  195.0 29.6 %copy-start.12 = (f32[1024]{0:T(1024)S(1)}, f32[1024]{0:T(1024)}, u32[]{:S(2)}) copy-start(f32[1024]{0:T(1024)} %param.27) | copy-start | bytes 12292
  195.0 30.9 %copy-start.14 = (f32[1024]{0:T(1024)S(1)}, f32[1024]{0:T(1024)}, u32[]{:S(2)}) copy-start(f32[1024]{0:T(1024)} %param.28) | copy-start | bytes 12292
  195.0 59.8 %all-gather.18.cloned.1.call-start = ((), (), s32[]{:S(2)}) async-start(), calls=%async_computation.13 | async-start | bytes 1310720 | tf_op jit(solution)/shard_map/all_gather | solution.py:178
  228.1 61.4 %reduce-scatter.15.cloned.1.call-start = ((), (), s32[]{:S(2)}) async-start(), calls=%async_computation.14 | async-start | bytes 1310720 | tf_op jit(solution)/shard_map/reduce_scatter | solution.py:189
  254.9 5.6 %copy-start.15 = (bf16[1024,1024]{1,0:T(8,128)(2,1)S(1)}, bf16[1024,1024]{1,0:T(8,128)(2,1)}, u32[]{:S(2)}) copy-start(bf16[1024,1024]{1,0:T(8,128)(2,1)} %all-gather.14.cloned.1.call-done) | copy-start | bytes 6291460
  259.5 1.0 copy-start.19
  260.5 29.1 %copy-start.4 = (bf16[1,128,1024]{2,1,0:T(8,128)(2,1)S(1)}, bf16[1,128,1024]{2,1,0:T(8,128)(2,1)}, u32[]{:S(2)}) copy-start(bf16[1,128,1024]{2,1,0:T(8,128)(2,1)} %reduce-scatter.11.cloned.1.call-done) | copy-start | bytes 786436
  262.8 57.0 %all-gather.20.cloned.1.call-start = ((), (), s32[]{:S(2)}) async-start(), calls=%async_computation.15 | async-start | bytes 1310720 | tf_op jit(solution)/shard_map/all_gather | solution.py:199
  293.0 100.4 %reduce-scatter.17.cloned.1.call-start = ((), (), s32[]{:S(2)}) async-start(), calls=%async_computation.16 | async-start | bytes 1310720 | tf_op jit(solution)/shard_map/reduce_scatter | solution.py:218
  321.4 3.5 copy-start.1
  328.6 1.4 copy-start.6
  330.0 2.2 copy-start.18
  332.2 2.7 copy-start.17
  332.2 80.6 %reduce-scatter.21.cloned.1.call-start = ((), (), s32[]{:S(2)}) async-start(), calls=%async_computation.18 | async-start | bytes 4718592
  332.2 2.7 copy-start.20
  345.1 1.2 copy-start.7
  345.1 1.7 copy-start.16
  345.2 112.5 %reduce-scatter.19.cloned.1.call-start = ((), (), s32[]{:S(2)}) async-start(), calls=%async_computation.17 | async-start | bytes 2359296
  350.6 42.8 %copy-start.5 = (f32[1,128,1024]{2,1,0:T(8,128)S(1)}, f32[1,128,1024]{2,1,0:T(8,128)}, u32[]{:S(2)}) copy-start(f32[1,128,1024]{2,1,0:T(8,128)} %get-tuple-element.118) | copy-start | bytes 1572868
Sparse Core Ops, SparseCore 0:
  9.9 28.3 all-gather.9
  39.9 27.9 all-gather.7
  76.0 26.6 reduce-scatter.10
  104.6 26.5 all-gather.13
  133.2 27.9 all-gather.11
  163.1 27.6 all-gather.15
  195.2 27.1 reduce-scatter.12
  228.2 26.5 all-gather.17
  262.9 26.6 reduce-scatter.14
  293.1 26.5 all-gather.19
  332.3 26.6 reduce-scatter.16
  362.2 50.5 reduce-scatter.20
  416.4 41.2 reduce-scatter.18

commit v2 on v1

--- a/solution.py
+++ b/solution.py
@@ -1,6 +1,10 @@
+import functools
+
 import jax
 import jax.numpy as jnp
 from jax import lax
+from jax.experimental import pallas as pl
+from jax.experimental.pallas import tpu as pltpu
 from jax.sharding import PartitionSpec as P
 
 HEADS = 16
@@ -52,6 +56,243 @@
         0.5 * (1.0 + lax.erf(preact * root_half))
         + preact * jnp.exp(-0.5 * preact * preact) * inv_root_tau
     )
+
+
+MESH = pl.DeviceIdType.MESH
+in_vmem = pl.BlockSpec(memory_space=pltpu.VMEM)
+row_chunks = 4
+
+
+def line_barrier(z, n):
+    barrier = pltpu.get_barrier_semaphore()
+    for there, other in ((z > 0, z - 1), (z < n - 1, z + 1)):
+
+        @pl.when(there)
+        def _():
+            pl.semaphore_signal(barrier, inc=1, device_id={"tensor": other}, device_id_type=MESH)
+
+    inner = (z > 0) & (z < n - 1)
+
+    @pl.when(inner)
+    def _():
+        pl.semaphore_wait(barrier, 2)
+
+    @pl.when(jnp.logical_not(inner))
+    def _():
+        pl.semaphore_wait(barrier, 1)
+
+
+class LineSum:
+    def __init__(self, z, n, part, stage, from_left, from_right, acc, send, recv):
+        self.z, self.n = z, n
+        self.part, self.stage, self.acc = part, stage, acc
+        self.bufs, self.send, self.recv = (from_left, from_right), send, recv
+        self.rows = part.shape[1] // row_chunks
+
+    def at(self, c):
+        return pl.ds(c * self.rows, self.rows)
+
+    def copy(self, way, d, c, src):
+        z, n = self.z, self.n
+        other = lax.rem(z + 1, n) if way == 0 else lax.rem(z + n - 1, n)
+        return pltpu.make_async_remote_copy(
+            src_ref=src.at[d, self.at(c)],
+            dst_ref=self.bufs[way].at[d, self.at(c)],
+            send_sem=self.send.at[way, d, c],
+            recv_sem=self.recv.at[way, d, c],
+            device_id={"tensor": other},
+            device_id_type=MESH,
+        )
+
+    def pairs(self):
+        for k in range(self.n - 1):
+            yield 0, self.n - 1 - k, self.z < self.n - 1 - k
+            yield 1, k, self.z > k
+
+    def start_ends(self):
+        for c in range(row_chunks):
+            for way, d, active in self.pairs():
+
+                @pl.when(self.z == (0 if way == 0 else self.n - 1))
+                def _():
+                    self.copy(way, d, c, self.part).start()
+
+    def forward(self, c):
+        for way, d, active in self.pairs():
+            inner = self.z > 0 if way == 0 else self.z < self.n - 1
+
+            @pl.when(active & inner)
+            def _():
+                self.copy(way, d, c, self.part).wait_recv()
+                at = self.at(c)
+                total = self.part[d, at].astype(jnp.float32) + self.bufs[way][d, at].astype(jnp.float32)
+                self.stage[d, at] = total.astype(jnp.bfloat16)
+                self.copy(way, d, c, self.stage).start()
+
+    def finish(self, c):
+        z, at = self.z, self.at(c)
+        self.acc[at] = self.part[z, at].astype(jnp.float32)
+        for way, there in ((0, z > 0), (1, z < self.n - 1)):
+
+            @pl.when(there)
+            def _():
+                self.copy(way, z, c, self.part).wait_recv()
+                self.acc[at] += self.bufs[way][z, at].astype(jnp.float32)
+
+        return self.acc[at]
+
+    def drain(self):
+        for c in range(row_chunks):
+            for way, d, active in self.pairs():
+
+                @pl.when(active)
+                def _():
+                    self.copy(way, d, c, self.part).wait_send()
+
+
+class LineGather:
+    def __init__(self, z, n, full, send, recv):
+        self.z, self.n, self.full, self.send, self.recv = z, n, full, send, recv
+        self.rows = full.shape[1] // row_chunks
+
+    def copy(self, way, s, c):
+        z, n = self.z, self.n
+        other = lax.rem(z + 1, n) if way == 0 else lax.rem(z + n - 1, n)
+        block = self.full.at[s, pl.ds(c * self.rows, self.rows)]
+        return pltpu.make_async_remote_copy(
+            src_ref=block,
+            dst_ref=block,
+            send_sem=self.send.at[way, s, c],
+            recv_sem=self.recv.at[s, c],
+            device_id={"tensor": other},
+            device_id_type=MESH,
+        )
+
+    def start(self, c):
+        for way, there in ((0, self.z < self.n - 1), (1, self.z > 0)):
+
+            @pl.when(there)
+            def _():
+                self.copy(way, self.z, c).start()
+
+    def forward(self, c):
+        for k in range(1, self.n):
+            for way, s, there, onward in (
+                (0, self.z - k, self.z >= k, self.z < self.n - 1),
+                (1, self.z + k, self.z < self.n - k, self.z > 0),
+            ):
+
+                @pl.when(there)
+                def _():
+                    self.copy(way, s, c).wait_recv()
+
+                    @pl.when(onward)
+                    def _():
+                        self.copy(way, s, c).start()
+
+    def drain(self):
+        for c in range(row_chunks):
+            for s in range(self.n):
+                for way, sent in (
+                    (0, (self.z >= s) & (self.z < self.n - 1)),
+                    (1, (self.z <= s) & (self.z > 0)),
+                ):
+
+                    @pl.when(sent)
+                    def _():
+                        self.copy(way, s, c).wait_send()
+
+
+def turn_kernel(n, middle, side_count, out_count, *refs):
+    part, side = refs[0], refs[1 : 1 + side_count]
+    full, outs = refs[1 + side_count], refs[2 + side_count : 2 + side_count + out_count]
+    stage, from_left, from_right, acc, sum_send, sum_recv, send, recv = refs[2 + side_count + out_count :]
+    z = lax.axis_index("tensor")
+    line_barrier(z, n)
+    summing = LineSum(z, n, part, stage, from_left, from_right, acc, sum_send, sum_recv)
+    gather = LineGather(z, n, full, send, recv)
+    summing.start_ends()
+    summing.forward(0)
+    for c in range(row_chunks):
+        if c + 1 < row_chunks:
+            summing.forward(c + 1)
+        total = summing.finish(c)
+        full[z, summing.at(c)] = middle(c, summing.at(c), total, side, outs)
+        gather.start(c)
+        if c > 0:
+            gather.forward(c - 1)
+    gather.forward(row_chunks - 1)
+    summing.drain()
+    gather.drain()
+
+
+def turn(n, number, name, middle, part, side, out_shapes):
+    shape = part.shape
+    return pl.pallas_call(
+        functools.partial(turn_kernel, n, middle, len(side), len(out_shapes)),
+        out_shape=[jax.ShapeDtypeStruct(shape, jnp.bfloat16)] + out_shapes,
+        in_specs=[in_vmem] * (1 + len(side)),
+        out_specs=[in_vmem] * (1 + len(out_shapes)),
+        scratch_shapes=[pltpu.VMEM(shape, jnp.bfloat16)] * 3
+        + [
+            pltpu.VMEM(shape[1:], jnp.float32),
+            pltpu.SemaphoreType.DMA((2, n, row_chunks)),
+            pltpu.SemaphoreType.DMA((2, n, row_chunks)),
+            pltpu.SemaphoreType.DMA((2, n, row_chunks)),
+            pltpu.SemaphoreType.DMA((n, row_chunks)),
+        ],
+        compiler_params=pltpu.CompilerParams(
+            collective_id=number, has_side_effects=True, vmem_limit_bytes=32 * 1024 * 1024
+        ),
+        cost_estimate=pl.CostEstimate(flops=60000000, bytes_accessed=40000000, transcendentals=0),
+        name=name,
+    )(part, *side)
+
+
+def add_small(ref, c, values):
+    for i, value in enumerate(values):
+        row = jnp.sum(value, axis=0, keepdims=True)
+        ref[i : i + 1] = row if c == 0 else ref[i : i + 1] + row
+
+
+def middle_one(c, at, total, side, outs):
+    layer_input, out_bias, gain, offset = side
+    unit_out, inv_out, low_out = outs
+    normed, unit, inv_std = norm_forward(
+        layer_input[at].astype(jnp.float32) + (total + out_bias[...]), gain[...], offset[...]
+    )
+    low_value = normed.astype(jnp.bfloat16)
+    unit_out[at] = unit
+    inv_out[at] = jnp.broadcast_to(inv_std, (inv_std.shape[0], 128))
+    low_out[at] = low_value
+    return low_value
+
+
+def middle_two(c, at, total, side, outs):
+    low_in, bias, gain, offset, upstream = side
+    output, resid_out, small = outs
+    result, unit, inv_std = norm_forward(
+        low_in[at].astype(jnp.float32) + (total + bias[...]), gain[...], offset[...]
+    )
+    output[at] = result.astype(jnp.bfloat16)
+    grad_top = upstream[at].astype(jnp.float32)
+    resid = norm_backward(grad_top, unit, inv_std, gain[...])
+    resid_out[at] = resid
+    branch = resid.astype(jnp.bfloat16)
+    add_small(small, c, (grad_top * unit, grad_top, branch.astype(jnp.float32)))
+    return branch
+
+
+def middle_three(c, at, total, side, outs):
+    resid_two, unit_one, inv_one, gain = side
+    resid_out, small = outs
+    grad_normed = total + resid_two[at]
+    unit = unit_one[at]
+    resid = norm_backward(grad_normed, unit, inv_one[at, 0:1], gain[...])
+    resid_out[at] = resid
+    branch = resid.astype(jnp.bfloat16)
+    add_small(small, c, (grad_normed * unit, grad_normed, branch.astype(jnp.float32)))
+    return branch
 
 
 def attend(operands):
@@ -142,62 +383,68 @@
     values = (packed[:, :, :, 2] + value_slice).astype(jnp.bfloat16)
     attended, log_total = lax.map(attend, (queries, key_rows, values))
     attended_rows = attended.reshape(row_count, width_here)
-    attn_part = matmul(attended_rows, out_full).reshape(seq_count, length, feature_count)
-    attn_branch = (
-        lax.psum_scatter(
-            attn_part.astype(jnp.bfloat16), "tensor", scatter_dimension=1, tiled=True
-        ).astype(jnp.float32)
-        + out_bias
-    )
-    normed_one, unit_one, inv_std_one = norm_forward(
-        layer_input.astype(jnp.float32) + attn_branch, attn_norm_gain, attn_norm_bias
-    )
-    normed_low = normed_one.astype(jnp.bfloat16)
-    normed_full = lax.all_gather(normed_low, "tensor", axis=1, tiled=True)
-    normed_rows = normed_full.reshape(row_count, feature_count)
+    local_rows = seq_count * piece_len
+
+    def by_piece(rows):
+        rows = rows.astype(jnp.bfloat16).reshape(seq_count, tensor_parts, piece_len, feature_count)
+        return rows.swapaxes(0, 1).reshape(tensor_parts, local_rows, feature_count)
+
+    def by_row(pieces):
+        pieces = pieces.reshape(tensor_parts, seq_count, piece_len, feature_count)
+        return pieces.swapaxes(0, 1).reshape(row_count, feature_count)
+
+    wide = jax.ShapeDtypeStruct((local_rows, feature_count), jnp.float32)
+    low = jax.ShapeDtypeStruct((local_rows, feature_count), jnp.bfloat16)
+    sums = jax.ShapeDtypeStruct((3, feature_count), jnp.float32)
+    local_input = layer_input.reshape(local_rows, feature_count)
+    normed_pieces, unit_one, inv_std_one, normed_low = turn(
+        tensor_parts,
+        1,
+        "turn_one",
+        middle_one,
+        by_piece(matmul(attended_rows, out_full)),
+        (local_input, out_bias[None], attn_norm_gain[None], attn_norm_bias[None]),
+        [wide, jax.ShapeDtypeStruct((local_rows, 128), jnp.float32), low],
+    )
+    normed_rows = by_row(normed_pieces)
     inner_bias = lax.dynamic_slice_in_dim(ffn_in_bias, tensor_rank * hidden_here, hidden_here, 0)
     inner_pre = matmul(normed_rows, ffn_in_full) + inner_bias
     activated = gelu_exact(inner_pre).astype(jnp.bfloat16)
-    ffn_part = matmul(activated, ffn_out_full).reshape(seq_count, length, feature_count)
-    ffn_branch = (
-        lax.psum_scatter(
-            ffn_part.astype(jnp.bfloat16), "tensor", scatter_dimension=1, tiled=True
-        ).astype(jnp.float32)
-        + ffn_out_bias
-    )
-    output_f32, unit_two, inv_std_two = norm_forward(
-        normed_low.astype(jnp.float32) + ffn_branch, ffn_norm_gain, ffn_norm_bias
-    )
-    layer_output = output_f32.astype(jnp.bfloat16)
-    grad_top = grad_output.astype(jnp.float32)
-    grad_ffn_norm_gain = jnp.sum(grad_top * unit_two, axis=(0, 1))
-    grad_ffn_norm_bias = jnp.sum(grad_top, axis=(0, 1))
-    grad_resid_two = norm_backward(grad_top, unit_two, inv_std_two, ffn_norm_gain)
-    grad_branch_two = grad_resid_two.astype(jnp.bfloat16)
-    grad_ffn_out_bias = jnp.sum(grad_branch_two.astype(jnp.float32), axis=(0, 1))
-    branch_two_full = lax.all_gather(grad_branch_two, "tensor", axis=1, tiled=True)
-    branch_two_rows = branch_two_full.reshape(row_count, feature_count)
+    branch_two_pieces, layer_output, grad_resid_two, small_two = turn(
+        tensor_parts,
+        2,
+        "turn_two",
+        middle_two,
+        by_piece(matmul(activated, ffn_out_full)),
+        (
+            normed_low,
+            ffn_out_bias[None],
+            ffn_norm_gain[None],
+            ffn_norm_bias[None],
+            grad_output.reshape(local_rows, feature_count),
+        ),
+        [low, wide, sums],
+    )
+    layer_output = layer_output.reshape(layer_input.shape)
+    grad_ffn_norm_gain, grad_ffn_norm_bias, grad_ffn_out_bias = small_two
+    branch_two_rows = by_row(branch_two_pieces)
     grad_activated = matmul_by_transpose(branch_two_rows, ffn_out_full).astype(jnp.bfloat16)
     grad_ffn_out_local = transpose_matmul(branch_two_rows, activated)
     grad_inner = (grad_activated.astype(jnp.float32) * gelu_slope(inner_pre)).astype(jnp.bfloat16)
     inner_bias_grad = jnp.sum(grad_inner.astype(jnp.float32), axis=0)
     grad_ffn_in_local = transpose_matmul(normed_rows, grad_inner)
-    normed_part = matmul_by_transpose(grad_inner, ffn_in_full).reshape(
-        seq_count, length, feature_count
-    )
-    grad_normed = (
-        lax.psum_scatter(
-            normed_part.astype(jnp.bfloat16), "tensor", scatter_dimension=1, tiled=True
-        ).astype(jnp.float32)
-        + grad_resid_two
-    )
-    grad_attn_norm_gain = jnp.sum(grad_normed * unit_one, axis=(0, 1))
-    grad_attn_norm_bias = jnp.sum(grad_normed, axis=(0, 1))
-    grad_resid_one = norm_backward(grad_normed, unit_one, inv_std_one, attn_norm_gain)
-    grad_branch_one = grad_resid_one.astype(jnp.bfloat16)
-    grad_out_bias = jnp.sum(grad_branch_one.astype(jnp.float32), axis=(0, 1))
-    branch_one_full = lax.all_gather(grad_branch_one, "tensor", axis=1, tiled=True)
-    branch_one_rows = branch_one_full.reshape(row_count, feature_count)
+    branch_one_pieces, grad_resid_one, small_one = turn(
+        tensor_parts,
+        3,
+        "turn_three",
+        middle_three,
+        by_piece(matmul_by_transpose(grad_inner, ffn_in_full)),
+        (grad_resid_two, unit_one, inv_std_one, attn_norm_gain[None]),
+        [wide, sums],
+    )
+    grad_resid_one = grad_resid_one.reshape(layer_input.shape)
+    grad_attn_norm_gain, grad_attn_norm_bias, grad_out_bias = small_one
+    branch_one_rows = by_row(branch_one_pieces)
     grad_attended = (
         matmul_by_transpose(branch_one_rows, out_full)
         .astype(jnp.bfloat16)

time: 468 us -> 403 us (0.86)
  waiting for transfers between devices: 316 us -> 101 us
  Pallas kernels: 0 us -> 172 us
  other arithmetic: 19.6 us -> 7.8 us
  matrix products: 37 us -> 28.6 us
    pallas_call x0 -> x3, Pallas kernels: none -> 172 us  [turn(): pl.pallas_call(functools.partial(turn_kernel, n, middle, len(side), len(o...]
    all_gather x3 -> x0, waiting for transfers between devices: 83.4 us -> none  [the longest x1 30 us: body(): normed_full = lax.all_gather(normed_low, 'tensor', axis=1, tiled=True)]
    reduce_scatter x3 -> x0, waiting for transfers between devices: 80 us -> none  [the longest x1 27.2 us: body(): lax.psum_scatter(ffn_part.astype(jnp.bfloat16), 'tensor', scatter_dimensi...]
    all_gather x1, waiting for transfers between devices: 24.6 us -> 0.01 us  [body(): lax.all_gather(ffn_out_weight, 'dp', axis=1, tiled=True)]
    all_gather x1, waiting for transfers between devices: 23 us -> 0.02 us  [body(): lax.all_gather(ffn_in_weight, 'dp', axis=0, tiled=True)]
    reduce_sum x8 -> x0, other arithmetic: 11.4 us -> none  [the longest x2 2.3 us: norm_forward(): variance = jnp.mean(center * center, axis=-1, keepdims=True)]
    dot_general x4, matrix products: 10.6 us -> 5.9 us  [matmul_by_transpose(): lax.dot_general(first_op, second_op, (((1,), (1,)), ((), ())), preferred_...]
    unnamed x15 -> x9, waiting for transfers between devices: 61.9 us -> 58.7 us
  transfers between devices with their start and end apart: 13 -> 7, of which waited for: 12 -> 4; matrix products, arithmetic and copies ran while one was open for 8% -> 10% of each run, Pallas kernels for 0% -> 15%
where the time goes in v2:
time: 403 us
  Pallas kernels  172 us (43%)
  waiting for transfers between devices  101 us (25%)
  blocking collectives  50.5 us (13%)
  matrix products  28.6 us (7%)
  local copies, waits for them, and re-layouts  27.6 us (7%)
  between operations  14.7 us (4%)
  other arithmetic  7.8 us (2%)
    pallas_call x3, Pallas kernels, turn(): pl.pallas_call(functools.partial(turn_kernel, n, middle, len(side), len(o...  172 us
    unnamed x9, waiting for transfers between devices  58.7 us
    psum x1, blocking collectives, body(): lax.psum(jnp.concatenate(small).reshape(-1, 128), ('dp', 'tensor'))  38 us
    all_gather x1, waiting for transfers between devices, body(): input_full = lax.all_gather(layer_input, 'tensor', axis=1, tiled=True)  27.8 us
    unnamed x65, local copies, waits for them, and re-layouts  20 us
    all_gather x1, waiting for transfers between devices, body(): lax.all_gather(qkv_weight, 'dp', axis=0, tiled=True)  14.1 us
    all_gather x1, blocking collectives, body(): lax.all_gather(out_weight, 'dp', axis=1, tiled=True)  12.5 us
    dot_general x4, matrix products, matmul(): return jnp.dot(first_op, second_op, preferred_element_type=jnp.float32)  10.6 us
  transfers between devices with their start and end apart: 7, of which 4 were waited for; matrix products, arithmetic and copies ran while one was open for 10% of the time, Pallas kernels for 15%

profile of v2, /device:TPU:0, one launch (start us, length us, event | category | flops | bytes accessed | tf_op | source)
XLA Modules:
  0.0 402.5 jit_solution(11210633422566454128)
XLA Ops:
  7.2 0.7 all-gather.7.cloned.1.call-update
  8.0 0.7 all-gather.5.cloned.1.call-update
  8.7 0.7 all-gather.9.cloned.1.call-update
  10.0 0.8 reshape.131
  10.8 0.8 reshape.130
  11.5 0.7 dynamic_slice.29
  12.2 12.5 %all_gather.17 = bf16[256,1024]{1,0:T(8,128)(2,1)S(1)} all-gather(bf16[256,128]{1,0:T(8,128)(2,1)} %param.19), channel_id=1, replica_groups=mesh['dp'=8,'tensor'=4] {'dp'}, dimensions={1}, use_global_device_ids=true | all-gather | bytes 589824 | tf_op jit(solution)/shard_map/all_gather | solution.py:366
  24.7 14.1 %all-gather.7.cloned.1.call-done = bf16[1024,768]{1,0:T(8,128)(2,1)} async-done(((bf16[128,768]{1,0:T(8,128)(2,1)}), bf16[1024,768]{1,0:T(8,128)(2,1)}) %all-gather.7.cloned.1.call-update) | async-done | bytes 1572880 | tf_op jit(solution)/shard_map/all_gather | solution.py:364
  38.8 1.7 copy.45
  40.6 27.8 %all-gather.5.cloned.1.call-done = bf16[1,512,1024]{2,1,0:T(8,128)(2,1)} async-done(((bf16[1,128,1024]{2,1,0:T(8,128)(2,1)}), bf16[1,512,1024]{2,1,0:T(8,128)(2,1)}) %all-gather.5.cloned.1.call-update) | async-done | bytes 1048592 | tf_op jit(solution)/shard_map/all_gather | solution.py:372
  68.4 2.2 convolution_bitcast_fusion
  70.6 0.8 multiply_reduce_fusion.1
  71.4 0.7 fusion
  72.1 1.2 copy-done.10
  73.4 1.0 fusion.20
  75.1 58.4 %turn_one.1 = (bf16[4,128,1024]{2,1,0:T(8,128)(2,1)S(1)}, f32[128,1024]{1,0:T(8,128)S(1)}, f32[128,128]{1,0:T(8,128)S(1)}, bf16[128,1024]{1,0:T(8,128)(2,1)S(1)}) custom-call(bf16[4,128,1024]{2,1,0:T(8,128)(2,1)S(1)} %bitcast.138, bf16[128,1024]{1,0:T(8,128)(2,1)S(1)} %bitcast.141, f32[1,1024]{1,0:T(1,128)S(1)} %bitcast.148, f32[1,1024]{1,0:T(1,128)S(1)} %bitcast.146, ...), custom_call_target="tpu_custom_call" | custom-call | flops 60000000 | bytes 40000000 | tf_op jit(solution)/shard_map/turn_one/pallas_call | solution.py:231
  133.6 4.6 %multiply_convert_fusion.1 = (bf16[512,1024]{1,0:T(8,128)(2,1)}, f32[512,1024]{1,0:T(8,128)}) fusion(f32[1024]{0:T(1024)S(1)} %dynamic_slice.29, bf16[512,1024]{1,0:T(8,128)(2,1)S(1)} %bitcast.153, bf16[1024,1024]{1,0:T(8,128)(2,1)} %all-gather.9.cloned.1.call-done), kind=kOutput, calls=%fused_computation.20 | convolution fusion | flops 1076887552 | bytes 6295552 | tf_op jit(solution)/shard_map/dot_general | solution.py:21
  138.2 3.3 convolution_convert_fusion.6
  141.6 60.5 %turn_two.1 = (bf16[4,128,1024]{2,1,0:T(8,128)(2,1)S(1)}, bf16[128,1024]{1,0:T(8,128)(2,1)S(1)}, f32[128,1024]{1,0:T(8,128)S(1)}, f32[3,1024]{1,0:T(4,128)S(1)}) custom-call(bf16[4,128,1024]{2,1,0:T(8,128)(2,1)S(1)} %bitcast.142, bf16[128,1024]{1,0:T(8,128)(2,1)S(1)} %get-tuple-element.72.refs_1_, f32[1,1024]{1,0:T(1,128)S(1)} %bitcast.150, ...), custom_call_target="tpu_custom_call" | custom-call | flops 60000000 | bytes 40000000 | tf_op jit(solution)/shard_map/turn_two/pallas_call | solution.py:231
  202.1 2.1 convert_reduce_fusion
  204.3 1.3 convolution_convert_fusion.4
  205.6 53.3 %turn_three.1 = (bf16[4,128,1024]{2,1,0:T(8,128)(2,1)S(1)}, f32[128,1024]{1,0:T(8,128)S(1)}, f32[3,1024]{1,0:T(4,128)S(1)}) custom-call(bf16[4,128,1024]{2,1,0:T(8,128)(2,1)S(1)} %bitcast.143, f32[128,1024]{1,0:T(8,128)S(1)} %get-tuple-element.75.refs_1_, f32[128,1024]{1,0:T(8,128)S(1)} %get-tuple-element.76.refs_2_, ...), custom_call_target="tpu_custom_call" | custom-call | flops 60000000 | bytes 40000000 | tf_op jit(solution)/shard_map/turn_three/pallas_call | solution.py:231
  259.5 0.9 convert_reduce_fusion.1
  260.9 1.2 multiply_reduce_fusion
  262.1 1.2 multiply_convert_fusion
  263.3 0.8 fusion.21
  264.8 0.9 copy-done.19
  266.3 2.0 fusion.14
  268.8 2.4 fusion.13
  271.3 1.5 pad_maximum_fusion.1
  272.8 4.0 copy.58
  277.0 0.9 copy-done.9
  278.0 2.6 convolution_convert_fusion
  280.6 1.3 convolution_convert_fusion.1
  281.9 2.5 pad_maximum_fusion
  284.4 6.5 %copy.60 = bf16[1024,2048]{1,0:T(8,128)(2,1)} copy(bf16[1024,2048]{0,1:T(8,128)(2,1)} %pad_maximum_fusion) | data formatting | bytes 8388608
  291.9 38.0 %psum.7 = f32[96,128]{1,0:T(8,128)S(1)} all-reduce(f32[96,128]{1,0:T(8,128)S(1)} %bitcast.167), channel_id=1, replica_groups=mesh['dp'=8,'tensor'=4] {'dp','tensor'}, use_global_device_ids=true, to_apply=%region_8.9 | all-reduce | flops 12288 | bytes 98304 | tf_op jit(solution)/shard_map/psum | solution.py:509
  330.6 0.6 slice_bitcast_fusion.5
  331.2 1.7 fusion.28
  332.9 4.1 %reduce-scatter.10.cloned.1.call-done = bf16[128,1024]{1,0:T(8,128)(2,1)} async-done(((bf16[1024,1024]{1,0:T(8,128)(2,1)}), bf16[128,1024]{1,0:T(8,128)(2,1)}) %reduce-scatter.10.cloned.1.call-update) | async-done | bytes 262160
  337.0 1.1 copy.59
  338.2 0.9 copy.51
  339.1 0.7 slice_bitcast_fusion.3
  339.8 51.9 %reduce-scatter.12.cloned.1.call-done = bf16[128,2048]{1,0:T(8,128)(2,1)} async-done(((bf16[1024,2048]{1,0:T(8,128)(2,1)}), bf16[128,2048]{1,0:T(8,128)(2,1)}) %reduce-scatter.12.cloned.1.call-update) | async-done | bytes 524304
  391.7 1.3 copy.61
  393.1 1.0 copy.52
  394.1 0.8 slice_bitcast_fusion
  395.0 0.7 copy.74
  (94 shorter events, 6.3 us)
Async XLA Ops:
  7.2 31.7 %all-gather.7.cloned.1.call-start = ((), (), s32[]{:S(2)}) async-start(), calls=%async_computation.4 | async-start | bytes 1769472 | tf_op jit(solution)/shard_map/all_gather | solution.py:364
  7.9 60.5 %all-gather.5.cloned.1.call-start = ((), (), s32[]{:S(2)}) async-start(), calls=%async_computation.3 | async-start | bytes 1310720 | tf_op jit(solution)/shard_map/all_gather | solution.py:372
  8.7 124.9 %all-gather.9.cloned.1.call-start = ((), (), s32[]{:S(2)}) async-start(), calls=%async_computation.5 | async-start | bytes 2359296 | tf_op jit(solution)/shard_map/all_gather | solution.py:365
  9.4 128.8 %all-gather.11.cloned.1.call-start = ((), (), s32[]{:S(2)}) async-start(), calls=%async_computation.6 | async-start | bytes 2359296 | tf_op jit(solution)/shard_map/all_gather | solution.py:367
  10.0 321.2 %reduce-scatter.8.cloned.1.call-start = ((), (), s32[]{:S(2)}) async-start(), calls=%async_computation.7 | async-start | bytes 1310720 | tf_op jit(solution)/shard_map/reduce_scatter | solution.py:465
  24.7 49.7 %copy-start.14 = (bf16[256,1024]{1,0:T(8,128)(2,1)}, bf16[256,1024]{1,0:T(8,128)(2,1)S(1)}, u32[]{:S(2)}) copy-start(bf16[256,1024]{1,0:T(8,128)(2,1)S(1)} %all_gather.17) | copy-start | bytes 1572868
  70.6 1.5 copy-start.12
  71.4 1.9 copy-start.10
  73.4 1.7 copy-start
  73.4 1.7 copy-start.2
  73.4 1.7 copy-start.3
  73.4 1.7 copy-start.4
  74.4 0.7 copy-start.17
  138.2 3.4 copy-start.1
  138.2 3.4 copy-start.5
  138.2 3.4 copy-start.6
  138.2 3.4 copy-start.7
  138.2 63.9 %copy-start.21 = (bf16[1024,1024]{1,0:T(8,128)(2,1)S(1)}, bf16[1024,1024]{1,0:T(8,128)(2,1)}, u32[]{:S(2)}) copy-start(bf16[1024,1024]{1,0:T(8,128)(2,1)} %all-gather.11.cloned.1.call-done) | copy-start | bytes 6291460
  138.2 63.9 %copy-start.22 = (f32[512,1024]{1,0:T(8,128)S(1)}, f32[512,1024]{1,0:T(8,128)}, u32[]{:S(2)}) copy-start(f32[512,1024]{1,0:T(8,128)} %get-tuple-element.144) | copy-start | bytes 6291460
  202.1 2.2 copy-start.8
  202.1 2.2 copy-start.20
  204.3 1.3 copy-start.23
  204.3 55.2 %copy-start.11 = (f32[4,512,512]{1,2,0:T(8,128)S(1)}, f32[4,512,512]{1,2,0:T(8,128)}, u32[]{:S(2)}) copy-start(f32[4,512,512]{1,2,0:T(8,128)} %copy-done.10) | copy-start | bytes 12582916
  205.6 53.4 %copy-start.15 = (bf16[256,1024]{1,0:T(8,128)(2,1)S(1)}, bf16[256,1024]{1,0:T(8,128)(2,1)}, u32[]{:S(2)}) copy-start(bf16[256,1024]{1,0:T(8,128)(2,1)} %copy-done.14) | copy-start | bytes 1572868
  259.5 1.4 copy-start.13
  264.6 1.7 copy-start.16
  264.8 0.9 copy-start.19
  266.3 2.1 copy-start.18
  268.3 68.7 %reduce-scatter.10.cloned.1.call-start = ((), (), s32[]{:S(2)}) async-start(), calls=%async_computation.8 | async-start | bytes 2359296
  276.8 1.2 copy-start.9
  276.8 114.9 %reduce-scatter.12.cloned.1.call-start = ((), (), s32[]{:S(2)}) async-start(), calls=%async_computation.9 | async-start | bytes 4718592
  278.0 2.6 copy-start.24
Sparse Core Ops, SparseCore 0:
  9.9 28.8 all-gather.6
  40.4 27.9 all-gather.4
  70.3 27.3 all-gather.8
  99.4 28.1 all-gather.10
  268.4 25.0 reduce-scatter.7
  297.0 39.9 reduce-scatter.9
  340.4 51.3 reduce-scatter.11

commit v3 on v2

--- a/solution.py
+++ b/solution.py
@@ -293,6 +293,306 @@
     branch = resid.astype(jnp.bfloat16)
     add_small(small, c, (grad_normed * unit, grad_normed, branch.astype(jnp.float32)))
     return branch
+
+
+def place():
+    p = lax.axis_index("dp")
+    return p, lax.div(p, 2), lax.rem(p, 2), lax.axis_index("tensor")
+
+
+def send_to(src, dst, send, recv, **peer):
+    return pltpu.make_async_remote_copy(
+        src_ref=src, dst_ref=dst, send_sem=send, recv_sem=recv, device_id=peer, device_id_type=MESH
+    )
+
+
+def greet_dp(barrier, groups, q, core):
+    def signal(peer):
+        pl.semaphore_signal(barrier, inc=1, device_id={"dp": peer}, device_id_type=MESH)
+
+    signal(2 * q + 1 - core)
+
+    def one(j, carry):
+        signal(2 * lax.rem(q + j, groups) + core)
+        return carry
+
+    lax.fori_loop(1, groups, one, 0)
+
+
+def opening_kernel(n, groups, x, first, second, x_full, first_full, second_full, *sems):
+    p, q, core, z = place()
+    send, recv, straight, pair, passed, from_peer, from_pair = sems
+    weights = ((first, first_full), (second, second_full))
+    barrier = pltpu.get_barrier_semaphore()
+    greet_dp(barrier, groups, q, core)
+    for there, other in ((z > 0, z - 1), (z < n - 1, z + 1)):
+
+        @pl.when(there)
+        def _():
+            pl.semaphore_signal(barrier, inc=1, device_id={"tensor": other}, device_id_type=MESH)
+
+    inner = (z > 0) & (z < n - 1)
+
+    @pl.when(inner)
+    def _():
+        pl.semaphore_wait(barrier, groups + 2)
+
+    @pl.when(jnp.logical_not(inner))
+    def _():
+        pl.semaphore_wait(barrier, groups + 1)
+
+    def to_peer(w, j):
+        shard, full = weights[w]
+        peer = 2 * lax.rem(q + j, groups) + core
+        return send_to(shard, full.at[p], straight.at[w, j], from_peer.at[w, q], dp=peer)
+
+    def came(w, other):
+        shard, full = weights[w]
+        return send_to(
+            shard, full.at[2 * other + core], straight.at[w, 0], from_peer.at[w, other], dp=2 * q + 1 - core
+        )
+
+    def to_pair(w, other):
+        full = weights[w][1]
+        block = full.at[2 * other + core]
+        return send_to(block, block, passed.at[w, other], from_pair.at[w, other], dp=2 * q + 1 - core)
+
+    def own_to_pair(w):
+        shard, full = weights[w]
+        return send_to(shard, full.at[p], pair.at[w], from_pair.at[w, q], dp=2 * q + 1 - core)
+
+    def pair_came(w, other):
+        shard, full = weights[w]
+        return send_to(
+            shard, full.at[2 * other + 1 - core], pair.at[w], from_pair.at[w, other], dp=2 * q + 1 - core
+        )
+
+    gather = LineGather(z, n, x_full, send, recv)
+    x_full[z] = x[...]
+    for c in range(row_chunks):
+        gather.start(c)
+    for w in range(2):
+
+        def push(j, carry):
+            to_peer(w, j).start()
+            return carry
+
+        lax.fori_loop(1, groups, push, 0)
+        own_to_pair(w).start()
+    for w in range(2):
+        shard, full = weights[w]
+        full[p] = shard[...]
+    for c in range(row_chunks):
+        gather.forward(c)
+    for w in range(2):
+
+        def forward(j, carry):
+            other = lax.rem(q + groups - j, groups)
+            came(w, other).wait_recv()
+            to_pair(w, other).start()
+            return carry
+
+        lax.fori_loop(1, groups, forward, 0)
+    for w in range(2):
+
+        def collect(other, carry):
+            pair_came(w, other).wait_recv()
+            return carry
+
+        lax.fori_loop(0, groups, collect, 0)
+
+        def drain(j, carry):
+            to_peer(w, j).wait_send()
+            to_pair(w, lax.rem(q + groups - j, groups)).wait_send()
+            return carry
+
+        lax.fori_loop(1, groups, drain, 0)
+        own_to_pair(w).wait_send()
+    gather.drain()
+
+
+def opening(n, devices, x, first, second):
+    groups = devices // 2
+    dma = pltpu.SemaphoreType.DMA
+    low = jnp.bfloat16
+    return pl.pallas_call(
+        functools.partial(opening_kernel, n, groups),
+        out_shape=[
+            jax.ShapeDtypeStruct((n,) + x.shape, low),
+            jax.ShapeDtypeStruct((devices,) + first.shape, low),
+            jax.ShapeDtypeStruct((devices,) + second.shape, low),
+        ],
+        in_specs=[in_vmem] * 3,
+        out_specs=[in_vmem] * 3,
+        scratch_shapes=[
+            dma((2, n, row_chunks)),
+            dma((n, row_chunks)),
+            dma((2, groups)),
+            dma((2,)),
+            dma((2, groups)),
+            dma((2, groups)),
+            dma((2, groups)),
+        ],
+        compiler_params=pltpu.CompilerParams(
+            collective_id=4, has_side_effects=True, vmem_limit_bytes=32 * 1024 * 1024
+        ),
+        cost_estimate=pl.CostEstimate(flops=60000000, bytes_accessed=40000000, transcendentals=0),
+        name="opening",
+    )(x, first, second)
+
+
+def closing_kernel(n, groups, part, resid, grads, small, grad_input, total, small_all, *scratch):
+    stage, from_left, from_right, acc, pair_buf, mine, peer_buf, small_pair, small_sum = scratch[:9]
+    (
+        sum_send, sum_recv, pair_send, pair_recv, peer_send, peer_recv,
+        small_pair_send, small_pair_recv, small_send, small_recv, end_send, end_recv,
+    ) = scratch[9:]
+    p, q, core, z = place()
+    barrier = pltpu.get_barrier_semaphore()
+    greet_dp(barrier, groups, q, core)
+    for k in range(1, n):
+        pl.semaphore_signal(
+            barrier, inc=1, device_id={"tensor": lax.rem(z + k, n)}, device_id_type=MESH
+        )
+    pl.semaphore_wait(barrier, groups + n - 1)
+    sibling = 2 * q + 1 - core
+
+    def to_pair(other):
+        return send_to(
+            grads.at[2 * other + 1 - core], pair_buf.at[other], pair_send.at[other], pair_recv.at[other], dp=sibling
+        )
+
+    def to_peer(other):
+        return send_to(
+            mine.at[other], peer_buf.at[q], peer_send.at[other], peer_recv.at[q], dp=2 * other + core
+        )
+
+    def from_peer(other):
+        return send_to(
+            mine.at[other], peer_buf.at[other], peer_send.at[other], peer_recv.at[other], dp=2 * other + core
+        )
+
+    def small_to_peer(other):
+        return send_to(
+            small_sum.at[q], small_sum.at[q], small_send.at[other], small_recv.at[q], dp=2 * other + core
+        )
+
+    def small_from_peer(other):
+        return send_to(
+            small_sum.at[other], small_sum.at[other], small_send.at[other], small_recv.at[other], dp=2 * other + core
+        )
+
+    def small_on(k):
+        there = lax.rem(z + k, n)
+        return send_to(small_all.at[z], small_all.at[z], end_send.at[k], end_recv.at[z], tensor=there)
+
+    def small_came(k):
+        there = lax.rem(z + k, n)
+        return send_to(small_all.at[there], small_all.at[there], end_send.at[k], end_recv.at[there], tensor=there)
+
+    def others(body):
+        def one(j, carry):
+            body(lax.rem(q + j, groups))
+            return carry
+
+        lax.fori_loop(1, groups, one, 0)
+
+    small_pair_copy = send_to(small, small_pair, small_pair_send, small_pair_recv, dp=sibling)
+    small_pair_copy.start()
+    others(lambda other: to_pair(other).start())
+    to_pair(q).start()
+    line = LineSum(z, n, part, stage, from_left, from_right, acc, sum_send, sum_recv)
+    line.start_ends()
+    small_pair_copy.wait_recv()
+    small_sum[q] = small[...] + small_pair[...]
+    others(lambda other: small_to_peer(other).start())
+
+    def pass_on(other):
+        to_pair(other).wait_recv()
+        pair_total = grads[2 * other + core].astype(jnp.float32) + pair_buf[other].astype(jnp.float32)
+        mine[other] = pair_total.astype(jnp.bfloat16)
+        to_peer(other).start()
+
+    others(pass_on)
+    line.forward(0)
+    line.forward(1)
+    others(lambda other: small_from_peer(other).wait_recv())
+    plane = small_sum[0]
+    for other in range(1, groups):
+        plane = plane + small_sum[other]
+    small_all[z] = plane
+    for k in range(1, n):
+        small_on(k).start()
+    for c in range(row_chunks):
+        if c + 2 < row_chunks:
+            line.forward(c + 2)
+        at = line.at(c)
+        grad_input[at] = (line.finish(c) + resid[at]).astype(jnp.bfloat16)
+    to_pair(q).wait_recv()
+    total[...] = grads[p].astype(jnp.float32) + pair_buf[q].astype(jnp.float32)
+
+    def add_peer(other):
+        from_peer(other).wait_recv()
+        total[...] += peer_buf[other].astype(jnp.float32)
+
+    others(add_peer)
+    for k in range(1, n):
+        small_came(k).wait_recv()
+    line.drain()
+    small_pair_copy.wait_send()
+    to_pair(q).wait_send()
+
+    def drain(other):
+        to_pair(other).wait_send()
+        to_peer(other).wait_send()
+        small_to_peer(other).wait_send()
+
+    others(drain)
+    for k in range(1, n):
+        small_on(k).wait_send()
+
+
+def closing(n, devices, part, resid, grads, small):
+    groups = devices // 2
+    dma = pltpu.SemaphoreType.DMA
+    low, wide = jnp.bfloat16, jnp.float32
+    slab = grads.shape[1:]
+    return pl.pallas_call(
+        functools.partial(closing_kernel, n, groups),
+        out_shape=[
+            jax.ShapeDtypeStruct(resid.shape, low),
+            jax.ShapeDtypeStruct(slab, wide),
+            jax.ShapeDtypeStruct((n,) + small.shape, wide),
+        ],
+        in_specs=[in_vmem] * 4,
+        out_specs=[in_vmem] * 3,
+        scratch_shapes=[pltpu.VMEM(part.shape, low)] * 3
+        + [
+            pltpu.VMEM(part.shape[1:], wide),
+            pltpu.VMEM((groups,) + slab, low),
+            pltpu.VMEM((groups,) + slab, low),
+            pltpu.VMEM((groups,) + slab, low),
+            pltpu.VMEM(small.shape, wide),
+            pltpu.VMEM((groups,) + small.shape, wide),
+            dma((2, n, row_chunks)),
+            dma((2, n, row_chunks)),
+            dma((groups,)),
+            dma((groups,)),
+            dma((groups,)),
+            dma((groups,)),
+            dma(()),
+            dma(()),
+            dma((groups,)),
+            dma((groups,)),
+            dma((n,)),
+            dma((n,)),
+        ],
+        compiler_params=pltpu.CompilerParams(
+            collective_id=5, has_side_effects=True, vmem_limit_bytes=32 * 1024 * 1024
+        ),
+        cost_estimate=pl.CostEstimate(flops=60000000, bytes_accessed=40000000, transcendentals=0),
+        name="closing",
+    )(part, resid, grads, small)
 
 
 def attend(operands):
@@ -360,17 +660,31 @@
     heads_here = HEADS // tensor_parts
     width_here = heads_here * HD
     hidden_here = FF // tensor_parts
-    qkv_full, ffn_in_full, out_full, ffn_out_full = (
-        lax.all_gather(qkv_weight, "dp", axis=0, tiled=True),
+    dp_parts = lax.axis_size("dp")
+    ffn_in_full, ffn_out_full = (
         lax.all_gather(ffn_in_weight, "dp", axis=0, tiled=True),
-        lax.all_gather(out_weight, "dp", axis=1, tiled=True),
         lax.all_gather(ffn_out_weight, "dp", axis=1, tiled=True),
     )
     seq_count, piece_len, feature_count = layer_input.shape
     length = piece_len * tensor_parts
     row_count = seq_count * length
-    input_full = lax.all_gather(layer_input, "tensor", axis=1, tiled=True)
-    input_rows = input_full.reshape(row_count, feature_count)
+    local_rows = seq_count * piece_len
+
+    def by_piece(rows):
+        rows = rows.astype(jnp.bfloat16).reshape(seq_count, tensor_parts, piece_len, feature_count)
+        return rows.swapaxes(0, 1).reshape(tensor_parts, local_rows, feature_count)
+
+    def by_row(pieces):
+        pieces = pieces.reshape(tensor_parts, seq_count, piece_len, feature_count)
+        return pieces.swapaxes(0, 1).reshape(row_count, feature_count)
+
+    local_input = layer_input.reshape(local_rows, feature_count)
+    input_pieces, qkv_slots, out_slots = opening(
+        tensor_parts, dp_parts, local_input, qkv_weight, out_weight
+    )
+    input_rows = by_row(input_pieces)
+    qkv_full = qkv_slots.reshape(feature_count, 3 * width_here)
+    out_full = out_slots.swapaxes(0, 1).reshape(width_here, feature_count)
     packed = matmul(input_rows, qkv_full).reshape(seq_count, length, heads_here, 3, HD)
     query_slice = lax.dynamic_slice_in_dim(
         query_bias.reshape(HEADS, HD), tensor_rank * heads_here, heads_here, 0
@@ -383,20 +697,9 @@
     values = (packed[:, :, :, 2] + value_slice).astype(jnp.bfloat16)
     attended, log_total = lax.map(attend, (queries, key_rows, values))
     attended_rows = attended.reshape(row_count, width_here)
-    local_rows = seq_count * piece_len
-
-    def by_piece(rows):
-        rows = rows.astype(jnp.bfloat16).reshape(seq_count, tensor_parts, piece_len, feature_count)
-        return rows.swapaxes(0, 1).reshape(tensor_parts, local_rows, feature_count)
-
-    def by_row(pieces):
-        pieces = pieces.reshape(tensor_parts, seq_count, piece_len, feature_count)
-        return pieces.swapaxes(0, 1).reshape(row_count, feature_count)
-
     wide = jax.ShapeDtypeStruct((local_rows, feature_count), jnp.float32)
     low = jax.ShapeDtypeStruct((local_rows, feature_count), jnp.bfloat16)
     sums = jax.ShapeDtypeStruct((3, feature_count), jnp.float32)
-    local_input = layer_input.reshape(local_rows, feature_count)
     normed_pieces, unit_one, inv_std_one, normed_low = turn(
         tensor_parts,
         1,
@@ -433,16 +736,26 @@
     grad_inner = (grad_activated.astype(jnp.float32) * gelu_slope(inner_pre)).astype(jnp.bfloat16)
     inner_bias_grad = jnp.sum(grad_inner.astype(jnp.float32), axis=0)
     grad_ffn_in_local = transpose_matmul(normed_rows, grad_inner)
+    shard_rows = feature_count // dp_parts
+    ffn_local = jnp.concatenate(
+        (
+            grad_ffn_in_local.astype(jnp.bfloat16).reshape(dp_parts, shard_rows, hidden_here),
+            grad_ffn_out_local.astype(jnp.bfloat16).reshape(dp_parts, shard_rows, hidden_here),
+        ),
+        axis=1,
+    ).reshape(2 * feature_count, hidden_here)
+    normed_part = by_piece(matmul_by_transpose(grad_inner, ffn_in_full))
+    ffn_local, normed_part = lax.optimization_barrier((ffn_local, normed_part))
+    ffn_grads = lax.psum_scatter(ffn_local, "dp", scatter_dimension=0, tiled=True).astype(jnp.float32)
     branch_one_pieces, grad_resid_one, small_one = turn(
         tensor_parts,
         3,
         "turn_three",
         middle_three,
-        by_piece(matmul_by_transpose(grad_inner, ffn_in_full)),
+        normed_part,
         (grad_resid_two, unit_one, inv_std_one, attn_norm_gain[None]),
         [wide, sums],
     )
-    grad_resid_one = grad_resid_one.reshape(layer_input.shape)
     grad_attn_norm_gain, grad_attn_norm_bias, grad_out_bias = small_one
     branch_one_rows = by_row(branch_one_pieces)
     grad_attended = (
@@ -458,59 +771,51 @@
         row_count, 3 * width_here
     )
     grad_qkv_local = transpose_matmul(input_rows, grad_packed)
-    input_part = matmul_by_transpose(grad_packed, qkv_full).reshape(
-        seq_count, length, feature_count
-    )
-    grad_input = (
-        lax.psum_scatter(
-            input_part.astype(jnp.bfloat16), "tensor", scatter_dimension=1, tiled=True
-        ).astype(jnp.float32)
-        + grad_resid_one
-    ).astype(jnp.bfloat16)
-    low_kind = jnp.bfloat16
-    ffn_grads = lax.psum_scatter(
-        jnp.concatenate((grad_ffn_in_local.astype(low_kind), grad_ffn_out_local.astype(low_kind)), axis=1),
-        "dp",
-        scatter_dimension=0,
-        tiled=True,
-    ).astype(jnp.float32)
-    attn_grads = lax.psum_scatter(
-        jnp.concatenate((grad_qkv_local.astype(low_kind), grad_out_local.astype(low_kind)), axis=1),
-        "dp",
-        scatter_dimension=0,
-        tiled=True,
-    ).astype(jnp.float32)
-    grad_ffn_in_weight = ffn_grads[:, :hidden_here]
-    grad_ffn_out_weight = ffn_grads[:, hidden_here:].T
-    grad_qkv_weight = attn_grads[:, : 3 * width_here]
-    grad_out_weight = attn_grads[:, 3 * width_here :].T
     query_grad_here = jnp.sum(grad_queries.astype(jnp.float32), axis=(0, 1)).reshape(width_here)
     value_grad_here = jnp.sum(grad_values.astype(jnp.float32), axis=(0, 1)).reshape(width_here)
-    query_padded = lax.dynamic_update_slice_in_dim(
-        jnp.zeros((HEADS * HD,), jnp.float32), query_grad_here, tensor_rank * width_here, 0
-    )
-    value_padded = lax.dynamic_update_slice_in_dim(
-        jnp.zeros((HEADS * HD,), jnp.float32), value_grad_here, tensor_rank * width_here, 0
-    )
-    inner_padded = lax.dynamic_update_slice_in_dim(
-        jnp.zeros((FF,), jnp.float32), inner_bias_grad, tensor_rank * hidden_here, 0
-    )
-    small = (
-        query_padded,
-        value_padded,
+    pieces = (
+        query_grad_here,
+        value_grad_here,
+        inner_bias_grad,
         grad_out_bias,
         grad_attn_norm_gain,
         grad_attn_norm_bias,
-        inner_padded,
         grad_ffn_out_bias,
         grad_ffn_norm_gain,
         grad_ffn_norm_bias,
     )
-    flat = lax.psum(jnp.concatenate(small).reshape(-1, 128), ("dp", "tensor")).reshape(-1)
-    summed, at = [], 0
-    for member in small:
-        summed.append(flat[at : at + member.shape[0]])
-        at += member.shape[0]
+    small_size = sum(piece.shape[0] for piece in pieces)
+    small = jnp.pad(jnp.concatenate(pieces), (0, -small_size % 1024)).reshape(-1, 128)
+    attn_local = jnp.concatenate(
+        (grad_qkv_local.astype(jnp.bfloat16), grad_out_local.astype(jnp.bfloat16)), axis=1
+    ).reshape(dp_parts, shard_rows, 4 * width_here)
+    grad_input, attn_grads, small_all = closing(
+        tensor_parts,
+        dp_parts,
+        by_piece(matmul_by_transpose(grad_packed, qkv_full)),
+        grad_resid_one,
+        attn_local,
+        small,
+    )
+    grad_input = grad_input.reshape(layer_input.shape)
+    grad_ffn_in_weight = ffn_grads[:shard_rows]
+    grad_ffn_out_weight = ffn_grads[shard_rows:].T
+    grad_qkv_weight = attn_grads[:, : 3 * width_here]
+    grad_out_weight = attn_grads[:, 3 * width_here :].T
+    flat = small_all.reshape(tensor_parts, -1)
+    split = 2 * width_here + hidden_here
+    common = jnp.sum(flat[:, split:small_size], axis=0).reshape(6, feature_count)
+    summed = (
+        flat[:, :width_here].reshape(-1),
+        flat[:, width_here : 2 * width_here].reshape(-1),
+        common[0],
+        common[1],
+        common[2],
+        flat[:, 2 * width_here : split].reshape(-1),
+        common[3],
+        common[4],
+        common[5],
+    )
     return (
         layer_output,
         grad_input,

time: 403 us -> 325 us (0.81)
  waiting for transfers between devices: 101 us -> 1.42 us
  Pallas kernels: 172 us -> 234 us
  blocking collectives: 50.5 us -> 0 us
  matrix products: 28.6 us -> 37.4 us
    pallas_call x0 -> x2, Pallas kernels: none -> 69.3 us  [the longest x1 40.7 us: closing(): pl.pallas_call(functools.partial(closing_kernel, n, groups), out_shape=[j...]
    unnamed x9 -> x3, waiting for transfers between devices: 58.7 us -> 1.39 us
    all_gather x2 -> x0, waiting for transfers between devices: 41.9 us -> none  [the longest x1 27.8 us: body(): input_full = lax.all_gather(layer_input, 'tensor', axis=1, tiled=True)]
    psum x1 -> x0, blocking collectives: 38 us -> none  [body(): lax.psum(jnp.concatenate(small).reshape(-1, 128), ('dp', 'tensor'))]
    all_gather x1 -> x0, blocking collectives: 12.5 us -> none  [body(): lax.all_gather(out_weight, 'dp', axis=1, tiled=True)]
    unnamed x65 -> x80, local copies, waits for them, and re-layouts: 20 us -> 11.7 us
    pallas_call x3, Pallas kernels: 172 us -> 164 us  [turn(): pl.pallas_call(functools.partial(turn_kernel, n, middle, len(side), len(o...]
    reshape x0 -> x2, local copies, waits for them, and re-layouts: none -> 6.63 us  [the longest x1 6.62 us: body(): ffn_local = jnp.concatenate((grad_ffn_in_local.astype(jnp.bfloat16).resha...]
  transfers between devices with their start and end apart: 7 -> 3, of which waited for: 4 -> 0; matrix products, arithmetic and copies ran while one was open for 10% -> 13% of each run, Pallas kernels for 15% -> 55%
where the time goes in v3:
time: 325 us; the launch traced here: 324 us
  Pallas kernels  234 us (72%)
  matrix products  37.4 us (12%)
  local copies, waits for them, and re-layouts  29.8 us (9%)
  between operations  14.3 us (4%)
  other arithmetic  7.49 us (2%)
    pallas_call x3, Pallas kernels, turn(): pl.pallas_call(functools.partial(turn_kernel, n, middle, len(side), len(o...  164 us
    pallas_call x1, Pallas kernels, closing(): pl.pallas_call(functools.partial(closing_kernel, n, groups), out_shape=[j...  40.7 us
    pallas_call x1, Pallas kernels, opening(): pl.pallas_call(functools.partial(opening_kernel, n, groups), out_shape=[j...  28.6 us
    unnamed x80, local copies, waits for them, and re-layouts  11.7 us
    dot_general x4, matrix products, matmul(): return jnp.dot(first_op, second_op, preferred_element_type=jnp.float32)  10.1 us
    dot_general x4, matrix products, matmul_by_transpose(): lax.dot_general(first_op, second_op, (((1,), (1,)), ((), ())), preferred_...  9.79 us
    reshape x1, local copies, waits for them, and re-layouts, body(): ffn_local = jnp.concatenate((grad_ffn_in_local.astype(jnp.bfloat16).resha...  6.62 us
  transfers between devices with their start and end apart: 3, of which 0 were waited for; matrix products, arithmetic and copies ran while one was open for 13% of the time, Pallas kernels for 55%

profile of v3, /device:TPU:0, one launch (start us, length us, event | category | flops | bytes accessed | tf_op | source)
XLA Modules:
  0.0 324.2 jit_solution(1741954067374941726)
XLA Ops:
  7.2 0.7 all-gather.3.cloned.1.call-update
  8.0 0.7 all-gather.5.cloned.1.call-update
  8.7 0.8 reshape.164
  9.5 0.8 reshape.163
  10.2 0.9 copy-done.1
  11.2 0.9 copy-done.6
  12.1 0.8 copy-done.7
  12.9 28.6 %opening.1 = (bf16[4,128,1024]{2,1,0:T(8,128)(2,1)S(1)}, bf16[8,128,768]{2,1,0:T(8,128)(2,1)S(1)}, bf16[8,256,128]{2,1,0:T(8,128)(2,1)S(1)}) custom-call(bf16[128,1024]{1,0:T(8,128)(2,1)S(1)} %bitcast.141, bf16[128,768]{1,0:T(8,128)(2,1)S(1)} %copy-done.6, bf16[256,128]{1,0:T(8,128)(2,1)S(1)} %copy-done.7), custom_call_target="tpu_custom_call" | custom-call | flops 60000000 | bytes 40000000 | tf_op jit(solution)/shard_map/opening/pallas_call | solution.py:418
  41.6 1.2 copy.41
  42.8 1.6 copy.39
  44.5 0.7 dynamic_slice.29
  45.2 2.4 convolution_bitcast_fusion
  47.6 0.8 multiply_reduce_fusion.1
  48.4 0.7 fusion
  49.2 1.0 fusion.18
  51.2 53.8 %turn_one.1 = (bf16[4,128,1024]{2,1,0:T(8,128)(2,1)S(1)}, f32[128,1024]{1,0:T(8,128)S(1)}, f32[128,128]{1,0:T(8,128)S(1)}, bf16[128,1024]{1,0:T(8,128)(2,1)S(1)}) custom-call(bf16[4,128,1024]{2,1,0:T(8,128)(2,1)S(1)} %bitcast.137, bf16[128,1024]{1,0:T(8,128)(2,1)S(1)} %bitcast.142, f32[1,1024]{1,0:T(1,128)S(1)} %bitcast.152, f32[1,1024]{1,0:T(1,128)S(1)} %bitcast.150, ...), custom_call_target="tpu_custom_call" | custom-call | flops 60000000 | bytes 40000000 | tf_op jit(solution)/shard_map/turn_one/pallas_call | solution.py:231
  105.0 4.3 %multiply_convert_fusion.1 = (bf16[512,1024]{1,0:T(8,128)(2,1)S(1)}, f32[512,1024]{1,0:T(8,128)}) fusion(f32[1024]{0:T(1024)S(1)} %dynamic_slice.29, bf16[512,1024]{1,0:T(8,128)(2,1)S(1)} %bitcast.159, bf16[1024,1024]{1,0:T(8,128)(2,1)} %all-gather.3.cloned.1.call-done), kind=kOutput, calls=%fused_computation.20 | convolution fusion | flops 1076887552 | bytes 6295552 | tf_op jit(solution)/shard_map/dot_general | solution.py:21
  109.3 2.9 convolution_convert_fusion.6
  112.2 56.0 %turn_two.1 = (bf16[4,128,1024]{2,1,0:T(8,128)(2,1)S(1)}, bf16[128,1024]{1,0:T(8,128)(2,1)S(1)}, f32[128,1024]{1,0:T(8,128)S(1)}, f32[3,1024]{1,0:T(4,128)S(1)}) custom-call(bf16[4,128,1024]{2,1,0:T(8,128)(2,1)S(1)} %bitcast.143, bf16[128,1024]{1,0:T(8,128)(2,1)S(1)} %get-tuple-element.83.refs_1_, f32[1,1024]{1,0:T(1,128)S(1)} %bitcast.154, ...), custom_call_target="tpu_custom_call" | custom-call | flops 60000000 | bytes 40000000 | tf_op jit(solution)/shard_map/turn_two/pallas_call | solution.py:231
  168.3 1.3 convolution_convert_fusion
  170.1 0.6 copy-done.28
  170.7 2.7 convert_reduce_fusion
  173.4 1.3 convolution_convert_fusion.1
  174.7 2.4 pad_maximum_fusion
  177.2 6.6 %copy.55 = bf16[2048,1024]{0,1:T(8,128)(2,1)} copy(bf16[2048,1024]{1,0:T(8,128)(2,1)} %bitcast.163) | data formatting | bytes 8388608 | tf_op jit(solution)/shard_map/reshape | solution.py:746
  183.8 2.9 convolution_convert_fusion.4
  186.7 1.0 copy-done.4
  187.8 54.5 %turn_three.1 = (bf16[4,128,1024]{2,1,0:T(8,128)(2,1)S(1)}, f32[128,1024]{1,0:T(8,128)S(1)}, f32[3,1024]{1,0:T(4,128)S(1)}) custom-call(bf16[4,128,1024]{2,1,0:T(8,128)(2,1)S(1)} %bitcast.144, f32[128,1024]{1,0:T(8,128)S(1)} %copy-done.4, f32[128,1024]{1,0:T(8,128)S(1)} %get-tuple-element.88.refs_2_, f32[128,128]{1,0:T(8,128)S(1)} %get-tuple-element.89.refs_3_, ...), custom_call_target="tpu_custom_call" | custom-call | flops 60000000 | bytes 40000000 | tf_op jit(solution)/shard_map/turn_three/pallas_call | solution.py:231
  242.3 1.5 convolution_convert_fusion.9
  243.8 3.1 convert_reduce_fusion.1
  247.1 3.7 %multiply_reduce_fusion = (f32[4,512]{1,0:T(4,128)S(1)}, f32[4,512,512]{1,2,0:T(8,128)S(1)}) fusion(f32[4,512,512]{1,2,0:T(8,128)} %copy-done.16, f32[4,512]{1,0:T(4,128)S(1)} %log_add_fusion, bf16[512,4,64]{0,2,1:T(8,128)(2,1)S(1)} %bitcast.167, f32[1,512,4,3,64]{1,4,3,2,0:T(8,128)} %copy-done.19, f32[4,64]{1,0:T(4,128)S(1)} %copy-done.25), kind=kOutput, calls=%fused_computation.2 | convolution fusion | flops 138672128 | bytes 9192448 | tf_op jit(solution)/shard_map/while/body/eval_jaxpr/qhe,khe->hqk/dot_general | solution.py:619
  250.8 2.6 multiply_convert_fusion
  253.3 2.3 convert_reduce_fusion.2
  255.8 2.5 fusion.19
  258.5 0.8 copy-done.22
  260.1 1.0 convolution_convert_fusion.2
  261.1 1.5 pad_maximum_fusion.1
  262.7 2.9 copy.47
  265.7 2.7 convolution_convert_fusion.3
  268.4 40.7 %closing.1 = (bf16[128,1024]{1,0:T(8,128)(2,1)S(1)}, f32[128,1024]{1,0:T(8,128)S(1)}, f32[4,64,128]{2,1,0:T(8,128)S(1)}) custom-call(bf16[4,128,1024]{2,1,0:T(8,128)(2,1)S(1)} %bitcast.140, f32[128,1024]{1,0:T(8,128)S(1)} %get-tuple-element.91.resid, bf16[8,128,1024]{2,1,0:T(8,128)(2,1)S(1)} %bitcast.134, f32[64,128]{1,0:T(8,128)S(1)} %pad_bitcast_fusion.small), custom_call_target="tpu_custom_call" | custom-call | flops 60000000 | bytes 40000000 | tf_op jit(solution)/shard_map/closing/pallas_call | solution.py:560
  311.0 0.8 slice.61
  311.8 0.8 copy.48
  312.6 0.6 fusion.35
  313.3 1.1 slice.84
  314.3 1.0 copy.49
  315.4 0.8 slice_bitcast_fusion
  316.2 0.7 copy.75
  316.9 0.7 copy.76
  (93 shorter events, 4.9 us)
Async XLA Ops:
  7.2 97.8 %all-gather.3.cloned.1.call-start = ((), (), s32[]{:S(2)}) async-start(), calls=%async_computation.1 | async-start | bytes 2359296 | tf_op jit(solution)/shard_map/all_gather | solution.py:665
  7.9 101.4 %all-gather.5.cloned.1.call-start = ((), (), s32[]{:S(2)}) async-start(), calls=%async_computation.2 | async-start | bytes 2359296 | tf_op jit(solution)/shard_map/all_gather | solution.py:666
  8.7 304.6 %reduce-scatter.2.cloned.1.call-start = ((), (), s32[]{:S(2)}) async-start(), calls=%async_computation.3 | async-start | bytes 4718592 | tf_op jit(solution)/shard_map/reduce_scatter | solution.py:749
  10.2 0.9 copy-start.1
  11.2 0.9 copy-start.6
  12.1 0.8 copy-start.7
  41.6 2.9 copy-start
  41.6 3.6 %copy-start.14 = (bf16[4,128,1024]{2,1,0:T(8,128)(2,1)}, bf16[4,128,1024]{2,1,0:T(8,128)(2,1)S(1)}, u32[]{:S(2)}) copy-start(bf16[4,128,1024]{2,1,0:T(8,128)(2,1)S(1)} %get-tuple-element.79) | copy-start | bytes 3145732
  45.2 4.0 %copy-start.24 = (f32[4,64]{1,0:T(4,128)}, f32[4,64]{1,0:T(4,128)S(1)}, u32[]{:S(2)}) copy-start(f32[4,64]{1,0:T(4,128)S(1)} %get-tuple-element.155) | copy-start | bytes 3076
  47.6 1.5 copy-start.19
  48.4 2.0 copy-start.16
  49.2 1.4 copy-start.18
  49.2 2.0 copy-start.2
  49.2 2.0 copy-start.8
  49.2 1.9 copy-start.9
  49.2 1.9 copy-start.10
  50.4 0.7 copy-start.21
  109.3 2.9 copy-start.5
  109.3 2.9 copy-start.11
  109.3 2.9 copy-start.12
  109.3 2.9 copy-start.13
  168.3 1.3 copy-start.3
  168.3 1.8 copy-start.27
  168.3 2.4 copy-start.28
  173.4 1.3 copy-start.29
  177.1 6.6 %copy-start.30 = (bf16[512,1024]{1,0:T(8,128)(2,1)S(1)}, bf16[512,1024]{1,0:T(8,128)(2,1)}, u32[]{:S(2)}) copy-start(bf16[512,1024]{1,0:T(8,128)(2,1)} %copy-done.29) | copy-start | bytes 3145732
  186.7 1.0 copy-start.4
  243.8 3.2 copy-start.25
  247.1 3.7 %copy-start.17 = (f32[4,512,512]{1,2,0:T(8,128)S(1)}, f32[4,512,512]{1,2,0:T(8,128)}, u32[]{:S(2)}) copy-start(f32[4,512,512]{1,2,0:T(8,128)} %copy-done.16) | copy-start | bytes 12582916
  258.3 1.0 copy-start.22
  258.4 1.7 copy-start.15
  259.3 0.9 copy-start.23
  262.7 2.9 copy-start.26
  313.3 2.1 copy-start.20
Sparse Core Ops, SparseCore 0:
  9.9 35.8 all-gather.2
  47.7 28.2 all-gather.4
  186.8 48.7 reduce-scatter.1

commit v4 on v3

--- a/solution.py
+++ b/solution.py
@@ -60,7 +60,7 @@
 
 MESH = pl.DeviceIdType.MESH
 in_vmem = pl.BlockSpec(memory_space=pltpu.VMEM)
-row_chunks = 4
+row_chunks = 2
 
 
 def line_barrier(z, n):
@@ -118,10 +118,18 @@
                     self.copy(way, d, c, self.part).start()
 
     def forward(self, c):
+        near_left = self.z < self.n // 2
+        self.forward_way(0, c, near_left)
+        self.forward_way(1, c, self.z >= 0)
+        self.forward_way(0, c, jnp.logical_not(near_left))
+
+    def forward_way(self, wanted, c, now):
         for way, d, active in self.pairs():
+            if way != wanted:
+                continue
             inner = self.z > 0 if way == 0 else self.z < self.n - 1
 
-            @pl.when(active & inner)
+            @pl.when(active & inner & now)
             def _():
                 self.copy(way, d, c, self.part).wait_recv()
                 at = self.at(c)
@@ -732,21 +740,17 @@
     grad_ffn_norm_gain, grad_ffn_norm_bias, grad_ffn_out_bias = small_two
     branch_two_rows = by_row(branch_two_pieces)
     grad_activated = matmul_by_transpose(branch_two_rows, ffn_out_full).astype(jnp.bfloat16)
-    grad_ffn_out_local = transpose_matmul(branch_two_rows, activated)
+    grad_ffn_out_local = transpose_matmul(activated, branch_two_rows)
     grad_inner = (grad_activated.astype(jnp.float32) * gelu_slope(inner_pre)).astype(jnp.bfloat16)
     inner_bias_grad = jnp.sum(grad_inner.astype(jnp.float32), axis=0)
     grad_ffn_in_local = transpose_matmul(normed_rows, grad_inner)
     shard_rows = feature_count // dp_parts
-    ffn_local = jnp.concatenate(
-        (
-            grad_ffn_in_local.astype(jnp.bfloat16).reshape(dp_parts, shard_rows, hidden_here),
-            grad_ffn_out_local.astype(jnp.bfloat16).reshape(dp_parts, shard_rows, hidden_here),
-        ),
-        axis=1,
-    ).reshape(2 * feature_count, hidden_here)
     normed_part = by_piece(matmul_by_transpose(grad_inner, ffn_in_full))
-    ffn_local, normed_part = lax.optimization_barrier((ffn_local, normed_part))
-    ffn_grads = lax.psum_scatter(ffn_local, "dp", scatter_dimension=0, tiled=True).astype(jnp.float32)
+    ffn_in_local, ffn_out_local, normed_part = lax.optimization_barrier(
+        (grad_ffn_in_local.astype(jnp.bfloat16), grad_ffn_out_local.astype(jnp.bfloat16), normed_part)
+    )
+    grad_ffn_in_weight = lax.psum_scatter(ffn_in_local, "dp", scatter_dimension=0, tiled=True).astype(jnp.float32)
+    grad_ffn_out_weight = lax.psum_scatter(ffn_out_local, "dp", scatter_dimension=1, tiled=True).astype(jnp.float32)
     branch_one_pieces, grad_resid_one, small_one = turn(
         tensor_parts,
         3,
@@ -798,8 +802,6 @@
         small,
     )
     grad_input = grad_input.reshape(layer_input.shape)
-    grad_ffn_in_weight = ffn_grads[:shard_rows]
-    grad_ffn_out_weight = ffn_grads[shard_rows:].T
     grad_qkv_weight = attn_grads[:, : 3 * width_here]
     grad_out_weight = attn_grads[:, 3 * width_here :].T
     flat = small_all.reshape(tensor_parts, -1)

time: 325 us -> 253 us (0.78)
  Pallas kernels: 234 us -> 164 us
    pallas_call x3, Pallas kernels: 164 us -> 112 us  [turn(): pl.pallas_call(functools.partial(turn_kernel, n, middle, len(side), len(o...]
    pallas_call x1, Pallas kernels: 40.7 us -> 25.8 us  [closing(): pl.pallas_call(functools.partial(closing_kernel, n, groups), out_shape=[j...]
    unnamed x80 -> x81, local copies, waits for them, and re-layouts: 11.7 us -> 18.9 us
    reshape x1 -> x0, local copies, waits for them, and re-layouts: 6.62 us -> none  [body(): ffn_local = jnp.concatenate((grad_ffn_in_local.astype(jnp.bfloat16).resha...]
    dot_general x4, matrix products: 4.01 us -> 7.94 us  [transpose_matmul(): lax.dot_general(first_op, second_op, (((0,), (0,)), ((), ())), preferred_...]
  transfers between devices with their start and end apart: 3 -> 4, of which waited for: 0 -> 1; matrix products, arithmetic and copies ran while one was open for 13% -> 15% of each run, Pallas kernels for 55% -> 50%
where the time goes in v4:
time: 253 us; the launch traced here: 252 us
  Pallas kernels  164 us (65%)
  matrix products  36.3 us (14%)
  local copies, waits for them, and re-layouts  27.3 us (11%)
  between operations  14.3 us (6%)
  other arithmetic  6.22 us (2%)
  waiting for transfers between devices  3.85 us (2%)
    pallas_call x3, Pallas kernels, turn(): pl.pallas_call(functools.partial(turn_kernel, n, middle, len(side), len(o...  112 us
    pallas_call x1, Pallas kernels, opening(): pl.pallas_call(functools.partial(opening_kernel, n, groups), out_shape=[j...  26.4 us
    pallas_call x1, Pallas kernels, closing(): pl.pallas_call(functools.partial(closing_kernel, n, groups), out_shape=[j...  25.8 us
    unnamed x81, local copies, waits for them, and re-layouts  18.9 us
    dot_general x4, matrix products, matmul(): return jnp.dot(first_op, second_op, preferred_element_type=jnp.float32)  10.9 us
    dot_general x4, matrix products, matmul_by_transpose(): lax.dot_general(first_op, second_op, (((1,), (1,)), ((), ())), preferred_...  9.67 us
    dot_general x4, matrix products, transpose_matmul(): lax.dot_general(first_op, second_op, (((0,), (0,)), ((), ())), preferred_...  7.94 us
  transfers between devices with their start and end apart: 4, of which 1 were waited for; matrix products, arithmetic and copies ran while one was open for 15% of the time, Pallas kernels for 50%

profile of v4, /device:TPU:0, one launch (start us, length us, event | category | flops | bytes accessed | tf_op | source)
XLA Modules:
  0.0 252.3 jit_solution(683796662598970110)
XLA Ops:
  7.2 0.7 all-gather.3.cloned.1.call-update
  8.0 0.7 all-gather.5.cloned.1.call-update
  8.7 0.9 copy-done.1
  9.7 0.9 copy-done.6
  10.6 0.8 copy-done.7
  11.5 26.4 %opening.1 = (bf16[4,128,1024]{2,1,0:T(8,128)(2,1)S(1)}, bf16[8,128,768]{2,1,0:T(8,128)(2,1)S(1)}, bf16[8,256,128]{2,1,0:T(8,128)(2,1)S(1)}) custom-call(bf16[128,1024]{1,0:T(8,128)(2,1)S(1)} %bitcast.138, bf16[128,768]{1,0:T(8,128)(2,1)S(1)} %copy-done.6, bf16[256,128]{1,0:T(8,128)(2,1)S(1)} %copy-done.7), custom_call_target="tpu_custom_call" | custom-call | flops 60000000 | bytes 40000000 | tf_op jit(solution)/shard_map/opening/pallas_call | solution.py:426
  37.9 2.0 copy.46
  40.1 1.0 copy.48
  41.1 0.7 dynamic_slice.29
  41.8 2.4 convolution_bitcast_fusion
  44.2 0.8 multiply_reduce_fusion.1
  45.0 0.7 fusion
  45.8 1.2 copy-done.16
  47.0 1.0 fusion.18
  48.7 38.9 %turn_one.1 = (bf16[4,128,1024]{2,1,0:T(8,128)(2,1)S(1)}, f32[128,1024]{1,0:T(8,128)S(1)}, f32[128,128]{1,0:T(8,128)S(1)}, bf16[128,1024]{1,0:T(8,128)(2,1)S(1)}) custom-call(bf16[4,128,1024]{2,1,0:T(8,128)(2,1)S(1)} %bitcast.134, bf16[128,1024]{1,0:T(8,128)(2,1)S(1)} %bitcast.139, f32[1,1024]{1,0:T(1,128)S(1)} %bitcast.149, f32[1,1024]{1,0:T(1,128)S(1)} %bitcast.147, ...), custom_call_target="tpu_custom_call" | custom-call | flops 60000000 | bytes 40000000 | tf_op jit(solution)/shard_map/turn_one/pallas_call | solution.py:239
  87.7 4.7 %multiply_convert_fusion.1 = (bf16[512,1024]{1,0:T(8,128)(2,1)}, f32[512,1024]{1,0:T(8,128)}) fusion(f32[1024]{0:T(1024)S(1)} %dynamic_slice.29, bf16[512,1024]{1,0:T(8,128)(2,1)S(1)} %bitcast.156, bf16[1024,1024]{1,0:T(8,128)(2,1)} %all-gather.3.cloned.1.call-done), kind=kOutput, calls=%fused_computation.19 | convolution fusion | flops 1076887552 | bytes 6295552 | tf_op jit(solution)/shard_map/dot_general | solution.py:21
  92.4 3.3 %convolution_convert_fusion.6 = bf16[512,1024]{1,0:T(8,128)(2,1)S(1)} fusion(bf16[512,1024]{1,0:T(8,128)(2,1)} %get-tuple-element.161, bf16[1024,1024]{1,0:T(8,128)(2,1)} %all-gather.5.cloned.1.call-done), kind=kOutput, calls=%fused_computation.29 | convolution fusion | flops 1074266112 | bytes 4194304 | tf_op jit(solution)/shard_map/dot_general | solution.py:21
  95.7 37.9 %turn_two.1 = (bf16[4,128,1024]{2,1,0:T(8,128)(2,1)S(1)}, bf16[128,1024]{1,0:T(8,128)(2,1)S(1)}, f32[128,1024]{1,0:T(8,128)S(1)}, f32[3,1024]{1,0:T(4,128)S(1)}) custom-call(bf16[4,128,1024]{2,1,0:T(8,128)(2,1)S(1)} %bitcast.140, bf16[128,1024]{1,0:T(8,128)(2,1)S(1)} %get-tuple-element.84.refs_1_, f32[1,1024]{1,0:T(1,128)S(1)} %bitcast.151, ...), custom_call_target="tpu_custom_call" | custom-call | flops 60000000 | bytes 40000000 | tf_op jit(solution)/shard_map/turn_two/pallas_call | solution.py:239
  133.7 2.7 %convolution_convert_fusion = bf16[1024,1024]{1,0:T(8,128)(2,1)} fusion(bf16[512,1024]{1,0:T(8,128)(2,1)S(1)} %copy-done.29, bf16[512,1024]{1,0:T(8,128)(2,1)S(1)} %bitcast.158), kind=kOutput, calls=%fused_computation.23 | convolution fusion | flops 1074790400 | bytes 4194304 | tf_op jit(solution)/shard_map/dot_general | solution.py:31
  136.4 2.1 convert_reduce_fusion
  138.5 1.0 copy-done.30
  139.5 2.7 %convolution_convert_fusion.1 = bf16[1024,1024]{1,0:T(8,128)(2,1)} fusion(bf16[512,1024]{1,0:T(8,128)(2,1)S(1)} %bitcast.157, bf16[512,1024]{1,0:T(8,128)(2,1)S(1)} %get-tuple-element.170), kind=kOutput, calls=%fused_computation.24 | convolution fusion | flops 1074790400 | bytes 4194304 | tf_op jit(solution)/shard_map/dot_general | solution.py:31
  142.2 3.2 %convolution_convert_fusion.4 = bf16[512,1024]{1,0:T(8,128)(2,1)S(1)} fusion(bf16[512,1024]{1,0:T(8,128)(2,1)} %copy-done.30, bf16[1024,1024]{1,0:T(8,128)(2,1)} %all-gather.3.cloned.1.call-done), kind=kOutput, calls=%fused_computation.27 | convolution fusion | flops 1074266112 | bytes 4194304 | tf_op jit(solution)/shard_map/dot_general | solution.py:25
  145.4 4.0 %copy.60 = bf16[1024,1024]{0,1:T(8,128)(2,1)} copy(bf16[1024,1024]{1,0:T(8,128)(2,1)} %convolution_convert_fusion) | data formatting | bytes 4194304
  149.5 1.0 copy-done.4
  150.5 35.2 %turn_three.1 = (bf16[4,128,1024]{2,1,0:T(8,128)(2,1)S(1)}, f32[128,1024]{1,0:T(8,128)S(1)}, f32[3,1024]{1,0:T(4,128)S(1)}) custom-call(bf16[4,128,1024]{2,1,0:T(8,128)(2,1)S(1)} %bitcast.141, f32[128,1024]{1,0:T(8,128)S(1)} %copy-done.4, f32[128,1024]{1,0:T(8,128)S(1)} %get-tuple-element.89.refs_2_, f32[128,128]{1,0:T(8,128)S(1)} %get-tuple-element.90.refs_3_, ...), custom_call_target="tpu_custom_call" | custom-call | flops 60000000 | bytes 40000000 | tf_op jit(solution)/shard_map/turn_three/pallas_call | solution.py:239
  185.7 1.5 convolution_convert_fusion.9
  187.2 3.8 %multiply_reduce_fusion = (f32[4,512]{1,0:T(4,128)S(1)}, f32[4,512,512]{1,2,0:T(8,128)S(1)}) fusion(f32[4,512,512]{1,2,0:T(8,128)} %copy-done.16, f32[4,512]{1,0:T(4,128)S(1)} %log_add_fusion, bf16[512,4,64]{0,2,1:T(8,128)(2,1)S(1)} %bitcast.163, f32[1,512,4,3,64]{1,4,3,2,0:T(8,128)} %copy-done.19, f32[4,64]{1,0:T(4,128)S(1)} %get-tuple-element.172), kind=kOutput, calls=%fused_computation.1 | convolution fusion | flops 138672128 | bytes 9192448 | tf_op jit(solution)/shard_map/while/body/eval_jaxpr/qhe,khe->hqk/dot_general | solution.py:627
  191.0 1.2 multiply_convert_fusion
  192.4 0.8 fusion.19
  193.8 0.9 convert_reduce_fusion.1
  194.9 0.9 copy-done.24
  196.2 2.2 convolution_convert_fusion.2
  198.4 0.9 copy-done.23
  199.8 1.0 copy-done.21
  200.7 1.5 pad_maximum_fusion
  202.3 2.9 %copy.53 = bf16[1024,1024]{1,0:T(8,128)(2,1)S(1)} copy(bf16[1024,1024]{0,1:T(8,128)(2,1)} %pad_maximum_fusion) | data formatting | bytes 4194304 | tf_op jit(solution)/shard_map/concatenate | solution.py:793
  205.5 2.8 %convolution_convert_fusion.3 = bf16[512,1024]{1,0:T(8,128)(2,1)S(1)} fusion(bf16[512,768]{0,1:T(8,128)(2,1)} %bitcast.171, bf16[1024,768]{1,0:T(8,128)(2,1)} %bitcast.136), kind=kOutput, calls=%fused_computation.26 | convolution fusion | flops 805830656 | bytes 3407872 | tf_op jit(solution)/shard_map/dot_general | solution.py:25
  208.3 25.8 %closing.1 = (bf16[128,1024]{1,0:T(8,128)(2,1)S(1)}, f32[128,1024]{1,0:T(8,128)S(1)}, f32[4,64,128]{2,1,0:T(8,128)S(1)}) custom-call(bf16[4,128,1024]{2,1,0:T(8,128)(2,1)S(1)} %bitcast.137, f32[128,1024]{1,0:T(8,128)S(1)} %get-tuple-element.92.resid, bf16[8,128,1024]{2,1,0:T(8,128)(2,1)S(1)} %bitcast.131, f32[64,128]{1,0:T(8,128)S(1)} %pad_bitcast_fusion.small), custom_call_target="tpu_custom_call" | custom-call | flops 60000000 | bytes 40000000 | tf_op jit(solution)/shard_map/closing/pallas_call | solution.py:568
  234.1 0.8 slice.55
  236.2 0.8 copy.54
  237.6 0.6 fusion.35
  238.2 1.1 copy.61
  239.3 0.8 convert_element_type.148
  240.2 2.4 reduce-scatter.5.cloned.1.call-done
  242.6 1.8 convert_element_type.147
  244.4 0.7 copy.81
  245.1 0.7 copy.82
  (94 shorter events, 5.1 us)
Async XLA Ops:
  7.2 32.7 %copy-start.25 = (f32[1024]{0:T(1024)S(1)}, f32[1024]{0:T(1024)}, u32[]{:S(2)}) copy-start(f32[1024]{0:T(1024)} %param.17) | copy-start | bytes 12292
  7.2 32.8 %copy-start.26 = (f32[1024]{0:T(1024)S(1)}, f32[1024]{0:T(1024)}, u32[]{:S(2)}) copy-start(f32[1024]{0:T(1024)} %param.18) | copy-start | bytes 12292
  7.2 80.5 %all-gather.3.cloned.1.call-start = ((), (), s32[]{:S(2)}) async-start(), calls=%async_computation.2 | async-start | bytes 2359296 | tf_op jit(solution)/shard_map/all_gather | solution.py:673
  7.9 84.5 %all-gather.5.cloned.1.call-start = ((), (), s32[]{:S(2)}) async-start(), calls=%async_computation.3 | async-start | bytes 2359296 | tf_op jit(solution)/shard_map/all_gather | solution.py:674
  8.7 229.5 %reduce-scatter.7.cloned.1.call-start = ((), (), s32[]{:S(2)}) async-start(), calls=%async_computation.5 | async-start | bytes 2359296
  8.7 1.0 copy-start.1
  9.7 0.9 copy-start.6
  10.6 0.8 copy-start.7
  37.9 3.2 %copy-start = (bf16[8,128,768]{2,1,0:T(8,128)(2,1)}, bf16[8,128,768]{2,1,0:T(8,128)(2,1)S(1)}, u32[]{:S(2)}) copy-start(bf16[8,128,768]{2,1,0:T(8,128)(2,1)S(1)} %get-tuple-element.81) | copy-start | bytes 4718596
  37.9 3.9 %copy-start.14 = (bf16[4,128,1024]{2,1,0:T(8,128)(2,1)}, bf16[4,128,1024]{2,1,0:T(8,128)(2,1)S(1)}, u32[]{:S(2)}) copy-start(bf16[4,128,1024]{2,1,0:T(8,128)(2,1)S(1)} %get-tuple-element.80) | copy-start | bytes 3145732
  44.2 1.5 copy-start.19
  45.0 2.0 copy-start.16
  47.0 1.0 copy-start.18
  47.0 1.7 copy-start.2
  47.0 1.7 copy-start.8
  47.0 1.7 copy-start.9
  47.0 1.7 copy-start.10
  48.0 0.7 copy-start.22
  92.4 3.3 %copy-start.5 = (bf16[1,128,1024]{2,1,0:T(8,128)(2,1)S(1)}, bf16[1,128,1024]{2,1,0:T(8,128)(2,1)}, u32[]{:S(2)}) copy-start(bf16[1,128,1024]{2,1,0:T(8,128)(2,1)} %param.29) | copy-start | bytes 786436
  92.4 3.3 %copy-start.11 = (f32[1024]{0:T(1024)S(1)}, f32[1024]{0:T(1024)}, u32[]{:S(2)}) copy-start(f32[1024]{0:T(1024)} %param.26) | copy-start | bytes 12292
  92.4 3.3 %copy-start.12 = (f32[1024]{0:T(1024)S(1)}, f32[1024]{0:T(1024)}, u32[]{:S(2)}) copy-start(f32[1024]{0:T(1024)} %param.27) | copy-start | bytes 12292
  92.4 3.3 %copy-start.13 = (f32[1024]{0:T(1024)S(1)}, f32[1024]{0:T(1024)}, u32[]{:S(2)}) copy-start(f32[1024]{0:T(1024)} %param.28) | copy-start | bytes 12292
  92.4 41.2 %copy-start.29 = (bf16[512,1024]{1,0:T(8,128)(2,1)S(1)}, bf16[512,1024]{1,0:T(8,128)(2,1)}, u32[]{:S(2)}) copy-start(bf16[512,1024]{1,0:T(8,128)(2,1)} %get-tuple-element.161) | copy-start | bytes 3145732
  133.6 2.7 %copy-start.3 = (f32[128,1024]{1,0:T(8,128)}, f32[128,1024]{1,0:T(8,128)S(1)}, u32[]{:S(2)}) copy-start(f32[128,1024]{1,0:T(8,128)S(1)} %get-tuple-element.88.refs_1_) | copy-start | bytes 1572868
  133.7 2.7 %copy-start.27 = (bf16[1024,1024]{1,0:T(8,128)(2,1)S(1)}, bf16[1024,1024]{1,0:T(8,128)(2,1)}, u32[]{:S(2)}) copy-start(bf16[1024,1024]{1,0:T(8,128)(2,1)} %all-gather.5.cloned.1.call-done) | copy-start | bytes 6291460
  133.7 2.7 %copy-start.28 = (f32[512,1024]{1,0:T(8,128)S(1)}, f32[512,1024]{1,0:T(8,128)}, u32[]{:S(2)}) copy-start(f32[512,1024]{1,0:T(8,128)} %get-tuple-element.162) | copy-start | bytes 6291460
  138.5 1.0 copy-start.30
  149.4 93.2 %reduce-scatter.5.cloned.1.call-start = ((), (), s32[]{:S(2)}) async-start(), calls=%async_computation.4 | async-start | bytes 2359296 | tf_op jit(solution)/shard_map/reduce_scatter | solution.py:752
  149.5 1.0 copy-start.4
  187.2 3.8 %copy-start.17 = (f32[4,512,512]{1,2,0:T(8,128)S(1)}, f32[4,512,512]{1,2,0:T(8,128)}, u32[]{:S(2)}) copy-start(f32[4,512,512]{1,2,0:T(8,128)} %copy-done.16) | copy-start | bytes 12582916
  191.0 1.4 copy-start.20
  194.7 1.5 copy-start.15
  194.9 0.9 copy-start.24
  198.4 0.9 copy-start.23
  199.3 1.4 copy-start.21
Sparse Core Ops, SparseCore 0:
  9.9 34.3 all-gather.2
  46.2 28.1 all-gather.4
  149.5 40.0 reduce-scatter.6
  198.5 44.0 reduce-scatter.4

commit v5 on v4

--- a/solution.py
+++ b/solution.py
@@ -739,15 +739,18 @@
     layer_output = layer_output.reshape(layer_input.shape)
     grad_ffn_norm_gain, grad_ffn_norm_bias, grad_ffn_out_bias = small_two
     branch_two_rows = by_row(branch_two_pieces)
+    grad_ffn_out_local = transpose_matmul(activated, branch_two_rows)
+    ffn_out_local, branch_two_rows = lax.optimization_barrier(
+        (grad_ffn_out_local.astype(jnp.bfloat16), branch_two_rows)
+    )
     grad_activated = matmul_by_transpose(branch_two_rows, ffn_out_full).astype(jnp.bfloat16)
-    grad_ffn_out_local = transpose_matmul(activated, branch_two_rows)
     grad_inner = (grad_activated.astype(jnp.float32) * gelu_slope(inner_pre)).astype(jnp.bfloat16)
     inner_bias_grad = jnp.sum(grad_inner.astype(jnp.float32), axis=0)
     grad_ffn_in_local = transpose_matmul(normed_rows, grad_inner)
     shard_rows = feature_count // dp_parts
     normed_part = by_piece(matmul_by_transpose(grad_inner, ffn_in_full))
-    ffn_in_local, ffn_out_local, normed_part = lax.optimization_barrier(
-        (grad_ffn_in_local.astype(jnp.bfloat16), grad_ffn_out_local.astype(jnp.bfloat16), normed_part)
+    ffn_in_local, normed_part = lax.optimization_barrier(
+        (grad_ffn_in_local.astype(jnp.bfloat16), normed_part)
     )
     grad_ffn_in_weight = lax.psum_scatter(ffn_in_local, "dp", scatter_dimension=0, tiled=True).astype(jnp.float32)
     grad_ffn_out_weight = lax.psum_scatter(ffn_out_local, "dp", scatter_dimension=1, tiled=True).astype(jnp.float32)

time: 253 us -> 254 us (level)
    dot_general x1, matrix products: 3.76 us -> 1.17 us  [attend_back(): jnp.einsum('qhe,khe->hqk', grad_attended, values, preferred_element_type=...]
    unnamed x81 -> x83, local copies, waits for them, and re-layouts: 18.9 us -> 18.3 us
  transfers between devices with their start and end apart: 4 -> 4, of which waited for: 1 -> 1; matrix products, arithmetic and copies ran while one was open for 15% -> 19% of each run, Pallas kernels for 50% -> 50%
where the time goes in v5:
time: 254 us; the launch traced here: 253 us
  Pallas kernels  164 us (65%)
  matrix products  35.8 us (14%)
  local copies, waits for them, and re-layouts  26.7 us (11%)
  between operations  14.3 us (6%)
  other arithmetic  7.61 us (3%)
  waiting for transfers between devices  4.44 us (2%)
    pallas_call x3, Pallas kernels, turn(): pl.pallas_call(functools.partial(turn_kernel, n, middle, len(side), len(o...  112 us
    pallas_call x1, Pallas kernels, opening(): pl.pallas_call(functools.partial(opening_kernel, n, groups), out_shape=[j...  26.4 us
    pallas_call x1, Pallas kernels, closing(): pl.pallas_call(functools.partial(closing_kernel, n, groups), out_shape=[j...  25.4 us
    unnamed x83, local copies, waits for them, and re-layouts  18.3 us
    dot_general x4, matrix products, matmul_by_transpose(): lax.dot_general(first_op, second_op, (((1,), (1,)), ((), ())), preferred_...  11.8 us
    dot_general x4, matrix products, matmul(): return jnp.dot(first_op, second_op, preferred_element_type=jnp.float32)  10.9 us
    dot_general x4, matrix products, transpose_matmul(): lax.dot_general(first_op, second_op, (((0,), (0,)), ((), ())), preferred_...  7.82 us
  transfers between devices with their start and end apart: 4, of which 1 were waited for; matrix products, arithmetic and copies ran while one was open for 19% of the time, Pallas kernels for 50%

profile of v5, /device:TPU:0, one launch (start us, length us, event | category | flops | bytes accessed | tf_op | source)
XLA Modules:
  0.0 253.2 jit_solution(12604383228769316809)
XLA Ops:
  7.2 0.7 all-gather.3.cloned.1.call-update
  8.0 0.7 all-gather.5.cloned.1.call-update
  8.8 0.9 copy-done.1
  9.7 0.9 copy-done.4
  10.6 0.8 copy-done.5
  11.5 26.4 %opening.1 = (bf16[4,128,1024]{2,1,0:T(8,128)(2,1)S(1)}, bf16[8,128,768]{2,1,0:T(8,128)(2,1)S(1)}, bf16[8,256,128]{2,1,0:T(8,128)(2,1)S(1)}) custom-call(bf16[128,1024]{1,0:T(8,128)(2,1)S(1)} %bitcast.138, bf16[128,768]{1,0:T(8,128)(2,1)S(1)} %copy-done.4, bf16[256,128]{1,0:T(8,128)(2,1)S(1)} %copy-done.5), custom_call_target="tpu_custom_call" | custom-call | flops 60000000 | bytes 40000000 | tf_op jit(solution)/shard_map/opening/pallas_call | solution.py:426
  37.9 2.0 copy.46
  40.1 1.0 copy.48
  41.1 0.7 dynamic_slice.29
  41.8 2.4 convolution_bitcast_fusion
  44.3 0.8 multiply_reduce_fusion.1
  45.1 0.7 fusion
  45.8 1.2 copy-done.15
  47.0 1.0 fusion.18
  48.8 38.9 %turn_one.1 = (bf16[4,128,1024]{2,1,0:T(8,128)(2,1)S(1)}, f32[128,1024]{1,0:T(8,128)S(1)}, f32[128,128]{1,0:T(8,128)S(1)}, bf16[128,1024]{1,0:T(8,128)(2,1)S(1)}) custom-call(bf16[4,128,1024]{2,1,0:T(8,128)(2,1)S(1)} %bitcast.134, bf16[128,1024]{1,0:T(8,128)(2,1)S(1)} %bitcast.139, f32[1,1024]{1,0:T(1,128)S(1)} %bitcast.149, f32[1,1024]{1,0:T(1,128)S(1)} %bitcast.147, ...), custom_call_target="tpu_custom_call" | custom-call | flops 60000000 | bytes 40000000 | tf_op jit(solution)/shard_map/turn_one/pallas_call | solution.py:239
  87.7 4.7 %multiply_convert_fusion.1 = (bf16[512,1024]{1,0:T(8,128)(2,1)}, f32[512,1024]{1,0:T(8,128)}) fusion(f32[1024]{0:T(1024)S(1)} %dynamic_slice.29, bf16[512,1024]{1,0:T(8,128)(2,1)S(1)} %bitcast.156, bf16[1024,1024]{1,0:T(8,128)(2,1)} %all-gather.3.cloned.1.call-done), kind=kOutput, calls=%fused_computation.19 | convolution fusion | flops 1076887552 | bytes 6295552 | tf_op jit(solution)/shard_map/dot_general | solution.py:21
  92.5 3.3 %convolution_convert_fusion.6 = bf16[512,1024]{1,0:T(8,128)(2,1)S(1)} fusion(bf16[512,1024]{1,0:T(8,128)(2,1)} %get-tuple-element.163, bf16[1024,1024]{1,0:T(8,128)(2,1)} %all-gather.5.cloned.1.call-done), kind=kOutput, calls=%fused_computation.29 | convolution fusion | flops 1074266112 | bytes 4194304 | tf_op jit(solution)/shard_map/dot_general | solution.py:21
  95.8 37.9 %turn_two.1 = (bf16[4,128,1024]{2,1,0:T(8,128)(2,1)S(1)}, bf16[128,1024]{1,0:T(8,128)(2,1)S(1)}, f32[128,1024]{1,0:T(8,128)S(1)}, f32[3,1024]{1,0:T(4,128)S(1)}) custom-call(bf16[4,128,1024]{2,1,0:T(8,128)(2,1)S(1)} %bitcast.140, bf16[128,1024]{1,0:T(8,128)(2,1)S(1)} %get-tuple-element.85.refs_1_, f32[1,1024]{1,0:T(1,128)S(1)} %bitcast.151, ...), custom_call_target="tpu_custom_call" | custom-call | flops 60000000 | bytes 40000000 | tf_op jit(solution)/shard_map/turn_two/pallas_call | solution.py:239
  133.7 1.0 copy-done.14
  134.7 2.6 %convolution_convert_fusion.1 = bf16[1024,1024]{1,0:T(8,128)(2,1)} fusion(bf16[512,1024]{1,0:T(8,128)(2,1)S(1)} %copy-done.30, bf16[512,1024]{1,0:T(8,128)(2,1)S(1)} %bitcast.158), kind=kOutput, calls=%fused_computation.24 | convolution fusion | flops 1074790400 | bytes 4194304 | tf_op jit(solution)/shard_map/dot_general | solution.py:31
  137.3 4.0 %copy.60 = bf16[1024,1024]{0,1:T(8,128)(2,1)} copy(bf16[1024,1024]{1,0:T(8,128)(2,1)} %convolution_convert_fusion.1) | data formatting | bytes 4194304
  141.4 0.6 copy-done.29
  142.0 5.0 %convert_reduce_fusion = (f32[1024]{0:T(1024)}, bf16[512,1024]{1,0:T(8,128)(2,1)S(1)}) fusion(f32[512,1024]{1,0:T(8,128)} %get-tuple-element.164, f32[1024]{0:T(1024)S(1)} %copy-done.29, bf16[512,1024]{1,0:T(8,128)(2,1)} %bitcast.159, bf16[1024,1024]{1,0:T(8,128)(2,1)} %all-gather.5.cloned.1.call-done), kind=kOutput, calls=%fused_computation.17 | convolution fusion | flops 1081605120 | bytes 6299648 | tf_op jit(solution)/shard_map/dot_general | solution.py:25
  147.0 1.0 copy-done.31
  148.0 2.7 %convolution_convert_fusion = bf16[1024,1024]{1,0:T(8,128)(2,1)} fusion(bf16[512,1024]{1,0:T(8,128)(2,1)S(1)} %bitcast.157, bf16[512,1024]{1,0:T(8,128)(2,1)S(1)} %get-tuple-element.172), kind=kOutput, calls=%fused_computation.23 | convolution fusion | flops 1074790400 | bytes 4194304 | tf_op jit(solution)/shard_map/dot_general | solution.py:31
  150.6 3.5 %convolution_convert_fusion.4 = bf16[512,1024]{1,0:T(8,128)(2,1)S(1)} fusion(bf16[512,1024]{1,0:T(8,128)(2,1)} %copy-done.31, bf16[1024,1024]{1,0:T(8,128)(2,1)} %all-gather.3.cloned.1.call-done), kind=kOutput, calls=%fused_computation.27 | convolution fusion | flops 1074266112 | bytes 4194304 | tf_op jit(solution)/shard_map/dot_general | solution.py:25
  154.2 35.6 %turn_three.1 = (bf16[4,128,1024]{2,1,0:T(8,128)(2,1)S(1)}, f32[128,1024]{1,0:T(8,128)S(1)}, f32[3,1024]{1,0:T(4,128)S(1)}) custom-call(bf16[4,128,1024]{2,1,0:T(8,128)(2,1)S(1)} %bitcast.141, f32[128,1024]{1,0:T(8,128)S(1)} %get-tuple-element.90.refs_1_, f32[128,1024]{1,0:T(8,128)S(1)} %get-tuple-element.91.refs_2_, ...), custom_call_target="tpu_custom_call" | custom-call | flops 60000000 | bytes 40000000 | tf_op jit(solution)/shard_map/turn_three/pallas_call | solution.py:239
  190.3 1.2 multiply_reduce_fusion
  191.4 1.2 multiply_convert_fusion
  192.6 0.8 fusion.19
  194.0 0.9 convert_reduce_fusion.1
  195.1 0.9 copy-done.22
  196.4 2.1 convolution_convert_fusion.2
  198.6 0.9 copy-done.21
  200.1 2.9 %pad_maximum_fusion = bf16[1024,1024]{0,1:T(8,128)(2,1)} fusion(bf16[1024,256]{0,1:T(8,128)(2,1)S(1)} %convolution_convert_fusion.8, bf16[1024,768]{0,1:T(8,128)(2,1)} %convolution_convert_fusion.2), kind=kLoop, calls=%fused_computation.16 | loop fusion | flops 4194304 | bytes 4194304 | tf_op jit(solution)/shard_map/concatenate | solution.py:796
  203.0 2.9 %copy.53 = bf16[1024,1024]{1,0:T(8,128)(2,1)S(1)} copy(bf16[1024,1024]{0,1:T(8,128)(2,1)} %pad_maximum_fusion) | data formatting | bytes 4194304 | tf_op jit(solution)/shard_map/concatenate | solution.py:796
  206.2 2.8 %convolution_convert_fusion.3 = bf16[512,1024]{1,0:T(8,128)(2,1)S(1)} fusion(bf16[512,768]{0,1:T(8,128)(2,1)} %bitcast.171, bf16[1024,768]{1,0:T(8,128)(2,1)} %bitcast.136), kind=kOutput, calls=%fused_computation.26 | convolution fusion | flops 805830656 | bytes 3407872 | tf_op jit(solution)/shard_map/dot_general | solution.py:25
  209.0 25.4 %closing.1 = (bf16[128,1024]{1,0:T(8,128)(2,1)S(1)}, f32[128,1024]{1,0:T(8,128)S(1)}, f32[4,64,128]{2,1,0:T(8,128)S(1)}) custom-call(bf16[4,128,1024]{2,1,0:T(8,128)(2,1)S(1)} %bitcast.137, f32[128,1024]{1,0:T(8,128)S(1)} %get-tuple-element.94.resid, bf16[8,128,1024]{2,1,0:T(8,128)(2,1)S(1)} %bitcast.131, f32[64,128]{1,0:T(8,128)S(1)} %pad_bitcast_fusion.small), custom_call_target="tpu_custom_call" | custom-call | flops 60000000 | bytes 40000000 | tf_op jit(solution)/shard_map/closing/pallas_call | solution.py:568
  234.4 0.8 slice.55
  235.2 0.8 copy.54
  236.0 0.6 copy.69
  237.9 0.6 fusion.35
  238.5 1.1 copy.61
  239.6 0.8 convert_element_type.148
  240.5 3.0 %reduce-scatter.5.cloned.1.call-done = bf16[128,1024]{1,0:T(8,128)(2,1)} async-done(((bf16[1024,1024]{1,0:T(8,128)(2,1)}), bf16[128,1024]{1,0:T(8,128)(2,1)}) %reduce-scatter.5.cloned.1.call-update) | async-done | bytes 262160 | tf_op jit(solution)/shard_map/reduce_scatter | solution.py:755
  243.5 1.8 convert_element_type.147
  245.3 0.7 copy.81
  246.0 0.7 copy.82
  (96 shorter events, 4.9 us)
Async XLA Ops:
  7.2 32.7 %copy-start.25 = (f32[1024]{0:T(1024)S(1)}, f32[1024]{0:T(1024)}, u32[]{:S(2)}) copy-start(f32[1024]{0:T(1024)} %param.18) | copy-start | bytes 12292
  7.2 32.8 %copy-start.26 = (f32[1024]{0:T(1024)S(1)}, f32[1024]{0:T(1024)}, u32[]{:S(2)}) copy-start(f32[1024]{0:T(1024)} %param.17) | copy-start | bytes 12292
  7.2 80.5 %all-gather.3.cloned.1.call-start = ((), (), s32[]{:S(2)}) async-start(), calls=%async_computation.2 | async-start | bytes 2359296 | tf_op jit(solution)/shard_map/all_gather | solution.py:673
  7.9 84.5 %all-gather.5.cloned.1.call-start = ((), (), s32[]{:S(2)}) async-start(), calls=%async_computation.3 | async-start | bytes 2359296 | tf_op jit(solution)/shard_map/all_gather | solution.py:674
  8.7 229.8 %reduce-scatter.7.cloned.1.call-start = ((), (), s32[]{:S(2)}) async-start(), calls=%async_computation.5 | async-start | bytes 2359296
  8.7 1.0 copy-start.1
  9.7 0.9 copy-start.4
  10.6 0.8 copy-start.5
  37.9 3.2 %copy-start = (bf16[8,128,768]{2,1,0:T(8,128)(2,1)}, bf16[8,128,768]{2,1,0:T(8,128)(2,1)S(1)}, u32[]{:S(2)}) copy-start(bf16[8,128,768]{2,1,0:T(8,128)(2,1)S(1)} %get-tuple-element.82) | copy-start | bytes 4718596
  37.9 3.9 %copy-start.12 = (bf16[4,128,1024]{2,1,0:T(8,128)(2,1)}, bf16[4,128,1024]{2,1,0:T(8,128)(2,1)S(1)}, u32[]{:S(2)}) copy-start(bf16[4,128,1024]{2,1,0:T(8,128)(2,1)S(1)} %get-tuple-element.81) | copy-start | bytes 3145732
  41.8 46.0 %copy-start.28 = (f32[1024]{0:T(1024)}, f32[1024]{0:T(1024)S(1)}, u32[]{:S(2)}) copy-start(f32[1024]{0:T(1024)S(1)} %dynamic_slice.29) | copy-start | bytes 12292
  41.8 4.0 %copy-start.23 = (f32[4,64]{1,0:T(4,128)}, f32[4,64]{1,0:T(4,128)S(1)}, u32[]{:S(2)}) copy-start(f32[4,64]{1,0:T(4,128)S(1)} %get-tuple-element.174) | copy-start | bytes 3076
  44.2 1.5 copy-start.18
  45.1 2.0 copy-start.15
  47.0 1.0 copy-start.17
  47.0 1.7 copy-start.2
  47.0 1.7 copy-start.6
  47.0 1.7 copy-start.7
  47.0 1.7 copy-start.8
  48.0 0.7 copy-start.20
  92.4 3.3 %copy-start.3 = (bf16[1,128,1024]{2,1,0:T(8,128)(2,1)S(1)}, bf16[1,128,1024]{2,1,0:T(8,128)(2,1)}, u32[]{:S(2)}) copy-start(bf16[1,128,1024]{2,1,0:T(8,128)(2,1)} %param.29) | copy-start | bytes 786436
  92.4 3.3 %copy-start.9 = (f32[1024]{0:T(1024)S(1)}, f32[1024]{0:T(1024)}, u32[]{:S(2)}) copy-start(f32[1024]{0:T(1024)} %param.26) | copy-start | bytes 12292
  92.4 3.3 %copy-start.10 = (f32[1024]{0:T(1024)S(1)}, f32[1024]{0:T(1024)}, u32[]{:S(2)}) copy-start(f32[1024]{0:T(1024)} %param.27) | copy-start | bytes 12292
  92.4 3.3 %copy-start.11 = (f32[1024]{0:T(1024)S(1)}, f32[1024]{0:T(1024)}, u32[]{:S(2)}) copy-start(f32[1024]{0:T(1024)} %param.28) | copy-start | bytes 12292
  92.5 42.2 %copy-start.30 = (bf16[512,1024]{1,0:T(8,128)(2,1)S(1)}, bf16[512,1024]{1,0:T(8,128)(2,1)}, u32[]{:S(2)}) copy-start(bf16[512,1024]{1,0:T(8,128)(2,1)} %get-tuple-element.163) | copy-start | bytes 3145732
  133.7 1.0 copy-start.14
  141.3 0.7 copy-start.29
  141.3 102.2 %reduce-scatter.5.cloned.1.call-start = ((), (), s32[]{:S(2)}) async-start(), calls=%async_computation.4 | async-start | bytes 2359296 | tf_op jit(solution)/shard_map/reduce_scatter | solution.py:755
  147.0 1.0 copy-start.31
  150.6 39.6 %copy-start.16 = (f32[4,512,512]{1,2,0:T(8,128)S(1)}, f32[4,512,512]{1,2,0:T(8,128)}, u32[]{:S(2)}) copy-start(f32[4,512,512]{1,2,0:T(8,128)} %copy-done.15) | copy-start | bytes 12582916
  154.1 36.1 %copy-start.19 = (f32[1,512,4,3,64]{1,4,3,2,0:T(8,128)S(1)}, f32[1,512,4,3,64]{1,4,3,2,0:T(8,128)}, u32[]{:S(2)}) copy-start(f32[1,512,4,3,64]{1,4,3,2,0:T(8,128)} %copy-done.18) | copy-start | bytes 4718596
  154.1 36.1 %copy-start.24 = (f32[4,64]{1,0:T(4,128)S(1)}, f32[4,64]{1,0:T(4,128)}, u32[]{:S(2)}) copy-start(f32[4,64]{1,0:T(4,128)} %copy-done.23) | copy-start | bytes 3076
  194.9 1.5 copy-start.13
  195.1 0.9 copy-start.22
  198.6 0.9 copy-start.21
  203.0 3.0 %copy-start.27 = (f32[1024]{0:T(1024)S(1)}, f32[1024]{0:T(1024)}, u32[]{:S(2)}) copy-start(f32[1024]{0:T(1024)} %get-tuple-element.171) | copy-start | bytes 12292
Sparse Core Ops, SparseCore 0:
  9.9 34.3 all-gather.2
  46.2 28.1 all-gather.4
  141.4 39.9 reduce-scatter.6
  198.7 44.7 reduce-scatter.4
